TPU v7x, 128 devices: a whole 4x4x4 slice. The times are simulated.
128 devices in a mesh: tm: 8 (over y, core), band: 16 (over x, z).
Axes of the slice: x: 4, y: 4, z: 4, core: 2. Of those that a mesh axis runs over, the one named last changes fastest.
Arguments:
- strain_rate: bfloat16 [32, 4096, 256], P('tm', 'band'), may hold values from -6 to 6
- pair_table: int32 [16, 8, 4], replicated, may hold values from 0 to 128, as said below
- pair_count: int32 [16], replicated, may hold values from 1 to 8, 64 in all
Outputs:
- xcorr: bfloat16 [16, 8, 256, 128, 128], P('band', 'tm')
Inputs may be any that keep to these rules, and one draw needn't show every extreme that they name: `pair_table`: columns 0 and 1 are blocks i and j with |i - j| <= 4; columns 2 and 3 are lo and hi with 1 <= lo < 16 and 96 <= hi <= 128; each owner's first slot has hi = 128. Slots at or past an owner's count hold valid entries too. Owner b's live slots are its first pair_count[b] slots; the counts sum to 64 and the largest equals 8.
All inputs are finite; a program needn't handle non-finite values.
Results may differ from a plain program's by a relative error of at most 0.0077.
Values may be sent and summed in bfloat16 or wider, within the bound.
A program may use at most 128 MiB of HBM per device.

v0:
```python
import math

import jax
import jax.numpy as jnp
from jax import lax
from jax.sharding import PartitionSpec as P

BLK = 128
SUB = 64


EPSILON = 1e-06


def forward_table(samples):
    position = jnp.arange(samples, dtype=jnp.int32)[:, None]
    harmonic = jnp.arange(samples // 2, dtype=jnp.int32)[None, :]
    angles = (position * harmonic % samples).astype(jnp.float32) * (2.0 * math.pi / samples)
    factor = 1.0 / math.sqrt(samples)
    return jnp.stack([jnp.cos(angles) * factor, -jnp.sin(angles) * factor], axis=1).astype(
        jnp.bfloat16
    )


def inverse_table(frequency, samples):
    delays = jnp.arange(samples, dtype=jnp.int32)[None, :]
    angles = (frequency[:, None] * delays % samples).astype(jnp.float32) * (2.0 * math.pi / samples)
    factor = 2.0 / math.sqrt(samples // 2)
    return jnp.stack([jnp.cos(angles) * factor, -jnp.sin(angles) * factor], axis=1).astype(
        jnp.bfloat16
    )


def whiten(strain_rate, groups):
    segments, channels, samples = strain_rate.shape
    bins_kept = samples // 2
    spectrum = jnp.einsum(
        "sgcl,lrk->ksgrc",
        strain_rate.reshape(segments, groups, BLK, samples),
        forward_table(samples),
        preferred_element_type=jnp.float32,
    )
    spectral_power = jnp.sum(spectrum * spectrum, axis=3)
    band_level = jnp.mean(
        spectral_power.reshape(bins_kept // SUB, SUB, segments, groups, BLK), axis=1
    )
    whitened = (
        spectrum.reshape(bins_kept // SUB, SUB, segments, groups, 2, BLK)
        / jnp.sqrt(band_level + EPSILON)[:, None, :, :, None, :]
    )
    return whitened.reshape(bins_kept, segments * groups, 2 * BLK).astype(jnp.bfloat16)


def block_rows(blocks, tm_count, segments, groups):
    owner_band = blocks // groups
    within_band = blocks % groups
    tm_slices = jnp.arange(tm_count, dtype=jnp.int32)[None, :, None]
    segment_pos = jnp.arange(segments, dtype=jnp.int32)[None, None, :]
    outer_index = owner_band[:, None, None] * tm_count + tm_slices
    row_index = (outer_index * segments + segment_pos) * groups + within_band[:, None, None]
    return row_index.reshape(blocks.shape[0], tm_count * segments)


def cross_block(spectrum_bin, bin_now, rows_left, rows_right, low_bins, high_bins, slot_weight):
    left_rows = jnp.take(spectrum_bin, rows_left, axis=0)
    right_rows = jnp.take(spectrum_bin, rows_right, axis=0)
    product = jnp.einsum("nsa,nsb->nab", left_rows, right_rows, preferred_element_type=jnp.float32)
    half_width = spectrum_bin.shape[1] // 2
    real_part = product[:, :half_width, :half_width] + product[:, half_width:, half_width:]
    imag_part = product[:, half_width:, :half_width] - product[:, :half_width, half_width:]
    inside = ((low_bins <= bin_now) & (bin_now < high_bins)).astype(jnp.float32) * slot_weight
    stacked = jnp.stack([real_part, imag_part], 1) * inside[:, None, None, None]
    return stacked.reshape(stacked.shape[0], 2, half_width * half_width).astype(jnp.bfloat16)


def correlate(received, table):
    lagged = jnp.einsum("kqnrx,krl->qnlx", received, table, preferred_element_type=jnp.float32)
    return lagged.astype(jnp.bfloat16)


def body(strain_rate, pair_table, pair_count):
    tm_count = lax.axis_size("tm")
    segments, channels, samples = strain_rate.shape
    groups = channels // BLK
    capacity = pair_table.shape[1]
    per_tm = capacity // tm_count
    whitened = whiten(strain_rate, groups)
    slot_index = jnp.arange(capacity, dtype=jnp.int32)
    weights = (slot_index[None, :] < pair_count[:, None]).astype(jnp.float32) / (
        segments * tm_count
    )
    band_local = lax.all_to_all(whitened, "tm", split_axis=0, concat_axis=1, tiled=True)
    gathered = lax.all_gather(band_local, "band", axis=1, tiled=True)
    band_id = lax.axis_index("band")
    owned_pairs = lax.dynamic_index_in_dim(pair_table, band_id, 0, keepdims=False)
    owned_weight = lax.dynamic_index_in_dim(weights, band_id, 0, keepdims=False)
    rows_left = block_rows(owned_pairs[:, 0], tm_count, segments, groups)
    rows_right = block_rows(owned_pairs[:, 1], tm_count, segments, groups)
    first_bin = lax.axis_index("tm") * gathered.shape[0]

    def per_bin(bin_args):
        spectrum_bin, offset = bin_args
        return cross_block(
            spectrum_bin,
            first_bin + offset,
            rows_left,
            rows_right,
            owned_pairs[:, 2],
            owned_pairs[:, 3],
            owned_weight,
        )

    cross_spec = lax.map(per_bin, (gathered, jnp.arange(gathered.shape[0], dtype=jnp.int32)))
    cross_spec = cross_spec.reshape(cross_spec.shape[0], tm_count, per_tm, 2, cross_spec.shape[-1])
    inverse = inverse_table(jnp.arange(samples // 2, dtype=jnp.int32), samples)
    result = correlate(
        lax.all_to_all(cross_spec, "tm", split_axis=1, concat_axis=0, tiled=True), table=inverse
    )
    return result.reshape(1, per_tm, samples, BLK, BLK)


def solution(mesh):
    placed = (P("tm", "band", None), P(), P())
    return jax.shard_map(
        body,
        mesh=mesh,
        in_specs=placed,
        out_specs=P("band", "tm", None, None, None),
        check_vma=False,
    )
```

profile of v0, /device:TPU:1, one launch (start us, length us, event | category | flops | bytes accessed | tf_op | source)
XLA Modules:
  0.0 355.1 jit_solution(7657250280633820428)
XLA Ops:
  8.5 1.8 div.44
  10.3 1.6 copy.64
  12.5 15.1 %all_to_all.33 = bf16[128,8,256]{2,1,0:T(8,128)(2,1)S(1)} all-to-all(bf16[128,8,256]{2,1,0:T(8,128)(2,1)S(1)} %copy.65), channel_id=1, replica_groups=mesh['tm'=8,'band'=16] {'tm'}, dimensions={0} | all-to-all | bytes 1048576 | tf_op jit(solution)/shard_map/all_to_all | solution.py:92
  30.0 70.3 %all-gather.2.cloned.1.call-done = bf16[16,1024,256]{2,1,0:T(8,128)(2,1)} async-done(((bf16[16,64,256]{2,1,0:T(8,128)(2,1)}), bf16[16,1024,256]{2,1,0:T(8,128)(2,1)}) %all-gather.2.cloned.1.call-update) | async-done | bytes 8388624 | tf_op jit(solution)/shard_map/all_gather | solution.py:93
  100.3 119.3 %while.12 = (s32[]{:T(128)}, bf16[16,8,2,16384]{3,2,0,1:T(2,128)(2,1)}, bf16[16,1024,256]{2,1,0:T(8,128)(2,1)}, s32[8,4]{0,1:T(4,128)S(1)}, s32[16]{0:T(128)S(1)...) while((s32[]{:T(128)}, ...), condition=%wide.region_3.5_spmd.clone.clone, body=%wide.region_2.4_spmd.clone.clone.sunk | while | flops 34740768 | bytes 11825661 | solution.py:113
  101.7 1.2 gather_fusion
  102.9 1.2 gather_fusion.1
  106.4 1.3 copy_dynamic-update-slice_fusion.2
  109.1 1.2 gather_fusion
  110.4 1.2 gather_fusion.1
  113.9 1.3 copy_dynamic-update-slice_fusion.2
  116.6 1.2 gather_fusion
  117.8 1.2 gather_fusion.1
  121.3 1.3 copy_dynamic-update-slice_fusion.2
  124.1 1.2 gather_fusion
  128.8 1.3 copy_dynamic-update-slice_fusion.2
  131.5 1.2 gather_fusion
  132.8 1.2 gather_fusion.1
  136.2 1.3 copy_dynamic-update-slice_fusion.2
  139.0 1.2 gather_fusion
  143.7 1.3 copy_dynamic-update-slice_fusion.2
  146.4 1.2 gather_fusion
  147.7 1.2 gather_fusion.1
  151.1 1.3 copy_dynamic-update-slice_fusion.2
  153.9 1.2 gather_fusion
  155.1 1.2 gather_fusion.1
  158.6 1.3 copy_dynamic-update-slice_fusion.2
  161.3 1.2 gather_fusion
  166.0 1.3 copy_dynamic-update-slice_fusion.2
  168.8 1.2 gather_fusion
  173.5 1.3 copy_dynamic-update-slice_fusion.2
  176.2 1.2 gather_fusion
  180.9 1.3 copy_dynamic-update-slice_fusion.2
  183.7 1.2 gather_fusion
  188.4 1.3 copy_dynamic-update-slice_fusion.2
  191.1 1.2 gather_fusion
  195.8 1.3 copy_dynamic-update-slice_fusion.2
  198.6 1.2 gather_fusion
  203.3 1.3 copy_dynamic-update-slice_fusion.2
  206.0 1.2 gather_fusion
  210.8 1.3 copy_dynamic-update-slice_fusion.2
  213.5 1.2 gather_fusion
  218.2 1.3 copy_dynamic-update-slice_fusion.2
  219.5 5.5 %all-to-all-start.1 = ((bf16[16,8,1,2,16384]{4,3,0,2,1:T(2,128)(2,1)}), bf16[16,8,1,2,16384]{4,3,0,2,1:T(2,128)(2,1)}, u32[]{:S(2)}, u32[]{:S(2)}) async-start(bf16[16,8,1,2,16384]{4,3,0,2,1:T(2,128)(2,1)} %bitcast.96), calls=%async_computation.1 | async-start | bytes 16777216 | tf_op jit(solution)/shard_map/all_to_all | solution.py:117
  225.6 93.3 %all-to-all-done.1 = bf16[16,8,1,2,16384]{4,3,0,2,1:T(2,128)(2,1)} async-done(((bf16[16,8,1,2,16384]{4,3,0,2,1:T(2,128)(2,1)}), bf16[16,8,1,2,16384]{4,3,0,2,1:T(2,128)(2,1)}, u32[]{:S(2)}, u32[]{:S(2)}) %all-to-all-start.1) | async-done | bytes 8388640 | tf_op jit(solution)/shard_map/all_to_all | solution.py:117
  318.9 12.1 %copy.69 = bf16[8,16,1,1,2,16384]{5,1,0,4,3,2:T(8,128)(2,1)} copy(bf16[8,16,1,1,2,16384]{5,4,1,0,3,2:T(2,128)(2,1)} %bitcast.16) | data formatting | bytes 16777216 | tf_op jit(solution)/shard_map/all_to_all | solution.py:117
  331.0 7.9 %fusion.13 = bf16[32,8,128,128]{3,1,2,0:T(8,128)(2,1)} fusion(bf16[128,2,16384]{2,0,1:T(8,128)(2,1)} %bitcast.93, bf16[128,1,256]{0,2,1:T(8,128)(2,1)S(1)} %get-tuple-element.164, bf16[128,1,256]{0,2,1:T(8,128)(2,1)S(1)} %get-tuple-element.165), kind=kOutput, calls=%fused_computation.26 | convolution fusion | flops 2151743488 | bytes 16908288 | tf_op jit(solution)/shard_map/kqnrx,krl->qnlx/dot_general | solution.py:77
  338.9 9.4 %copy.73 = bf16[32,8,128,128]{3,2,1,0:T(8,128)(2,1)} copy(bf16[32,8,128,128]{3,1,2,0:T(8,128)(2,1)} %fusion.13) | data formatting | bytes 16777216
  (313 shorter events, 67.9 us)
Async XLA Ops:
  6.5 1.0 copy-start
  6.5 93.7 %all-gather.2.cloned.1.call-start = ((), (), s32[]{:S(2)}) async-start(), calls=%async_computation.2 | async-start | bytes 8912896 | tf_op jit(solution)/shard_map/all_gather | solution.py:93
  7.6 21.0 %copy-start.1 = (s32[16,8,4]{0,2,1:T(4,128)S(1)}, s32[16,8,4]{0,2,1:T(4,128)}, u32[]{:S(2)}) copy-start(s32[16,8,4]{0,2,1:T(4,128)} %param.8) | copy-start | bytes 6148
  7.6 21.2 %copy-start.2 = (s32[16]{0:T(128)S(1)}, s32[16]{0:T(128)}, u32[]{:S(2)}) copy-start(s32[16]{0:T(128)} %param.9) | copy-start | bytes 196
  219.5 99.3 %all-to-all-start.1 = ((bf16[16,8,1,2,16384]{4,3,0,2,1:T(2,128)(2,1)}), bf16[16,8,1,2,16384]{4,3,0,2,1:T(2,128)(2,1)}, u32[]{:S(2)}, u32[]{:S(2)}) async-start(bf16[16,8,1,2,16384]{4,3,0,2,1:T(2,128)(2,1)} %bitcast.96), calls=%async_computation.1 | async-start | bytes 16777216 | tf_op jit(solution)/shard_map/all_to_all | solution.py:117
Sparse Core Ops, SparseCore 0:
  28.7 71.5 all-gather.1
where the time goes:
time: 356 us; the launch traced here: 355 us
  waiting for transfers between devices  164 us (46%)
  local copies, waits for them, and re-layouts  121 us (34%)
  matrix products  18.9 us (5%)
  blocking collectives  15.1 us (4%)
  between operations  13.5 us (4%)
  loops' own time  10 us (3%)
  other arithmetic  7.41 us (2%)
  starting transfers between devices  5.48 us (2%)
    all_to_all x1, waiting for transfers between devices, body(): lax.all_to_all(cross_spec, 'tm', split_axis=1, concat_axis=0, tiled=True)  93.3 us
    all_gather x1, waiting for transfers between devices, body(): gathered = lax.all_gather(band_local, 'band', axis=1, tiled=True)  70.3 us
    dynamic_update_slice x16, local copies, waits for them, and re-layouts, body(): lax.map(per_bin, (gathered, jnp.arange(gathered.shape[0], dtype=jnp.int32)))  21.4 us
    gather x16, local copies, waits for them, and re-layouts, cross_block(): right_rows = jnp.take(spectrum_bin, rows_right, axis=0)  18.4 us
    gather x16, local copies, waits for them, and re-layouts, cross_block(): left_rows = jnp.take(spectrum_bin, rows_left, axis=0)  18.4 us
    squeeze x16, local copies, waits for them, and re-layouts, body(): lax.map(per_bin, (gathered, jnp.arange(gathered.shape[0], dtype=jnp.int32)))  17.3 us
    all_to_all x1, blocking collectives, body(): lax.all_to_all(whitened, 'tm', split_axis=0, concat_axis=1, tiled=True)  15.1 us
    all_to_all x1, local copies, waits for them, and re-layouts, body(): lax.all_to_all(cross_spec, 'tm', split_axis=1, concat_axis=0, tiled=True)  12.1 us
  transfers between devices with their start and end apart: 2, of which 2 were waited for; matrix products, arithmetic and copies ran while one was open for 1% of the time, Pallas kernels for 0%

commit v1 on v0

v1 whole, which is shorter than its diff:
```python
import functools
import math

import jax
import jax.numpy as jnp
import numpy as np
from jax import lax
from jax.experimental import pallas as pl
from jax.experimental.pallas import tpu as pltpu
from jax.sharding import PartitionSpec as P

BLK = 128
SUB = 64
EPSILON = 1e-06
QUAD = 4
PAD = 136
BF = jnp.bfloat16


def forward_table(samples):
    n = np.arange(samples)[None, :]
    k = np.arange(samples // 2)[:, None]
    angles = (n * k % samples) * (2.0 * math.pi / samples)
    factor = 1.0 / math.sqrt(samples)
    table = np.concatenate([np.cos(angles) * factor, -np.sin(angles) * factor], axis=0)
    return jnp.asarray(table.astype(np.float32), dtype=BF)


def inverse_table(samples):
    k = np.arange(samples // 2)[None, :]
    t = np.arange(samples)[:, None]
    angles = (t * k % samples) * (2.0 * math.pi / samples)
    factor = 2.0 / math.sqrt(samples // 2)
    table = np.stack([np.cos(angles) * factor, -np.sin(angles) * factor], axis=2)
    return jnp.asarray(table.reshape(samples, samples).astype(np.float32), dtype=BF)


def whiten_kernel(strain_ref, table_ref, out_ref, rows_ref):
    segments, channels, samples = strain_ref.shape
    bins = samples // 2
    for g in range(channels // BLK):
        for s in range(segments):
            x = strain_ref[s, g * BLK : (g + 1) * BLK, :]
            spec = lax.dot_general(
                table_ref[...], x, (((1,), (1,)), ((), ())), preferred_element_type=jnp.float32
            )
            re, im = spec[:bins], spec[bins:]
            power = re * re + im * im
            for m in range(bins // SUB):
                cut = slice(m * SUB, (m + 1) * SUB)
                level = jnp.mean(power[cut], axis=0, keepdims=True)
                scale = 1.0 / jnp.sqrt(level + EPSILON)
                for r, part in enumerate((re, im)):
                    rows_ref[r, pl.ds(m * SUB * segments + s, SUB, stride=segments), :] = (
                        part[cut] * scale
                    )
        for r in range(2):
            out_ref[g, :, r] = rows_ref[r].reshape(bins // QUAD, QUAD * segments, BLK).astype(BF)


def whiten(strain_rate):
    segments, channels, samples = strain_rate.shape
    bins = samples // 2
    return pl.pallas_call(
        whiten_kernel,
        out_shape=jax.ShapeDtypeStruct(
            (channels // BLK, bins // QUAD, 2, QUAD * segments, BLK), BF
        ),
        in_specs=[pl.BlockSpec(memory_space=pltpu.VMEM)] * 2,
        out_specs=pl.BlockSpec(memory_space=pltpu.VMEM),
        scratch_shapes=[pltpu.VMEM((2, bins * segments, BLK), jnp.float32)],
    )(strain_rate, forward_table(samples))


def cross_quad(left, right, factors, planes_ref, first):
    depth = left.shape[0] * left.shape[1] * left.shape[2]
    left_t = left.reshape(depth, BLK).T
    bin_of = lax.broadcasted_iota(jnp.int32, left_t.shape, 1) % 16 // 4
    stacked = jnp.concatenate(
        [jnp.where(bin_of == q, left_t, jnp.zeros_like(left_t)) for q in range(QUAD)], axis=0
    )
    turned = jnp.stack([-right[:, 1], right[:, 0]], axis=1)
    both = jnp.concatenate([right.reshape(depth, BLK), turned.reshape(depth, BLK)], axis=1)
    product = jnp.dot(stacked, both, preferred_element_type=jnp.float32)
    for q in range(QUAD):
        for r in range(2):
            planes_ref[pl.ds((first + q * 2 + r) * PAD, BLK), :] = (
                product[q * BLK : (q + 1) * BLK, r * BLK : (r + 1) * BLK] * factors[q]
            )


def bin_factors(pair_ref, first_bin, segments):
    lo, hi, live = pair_ref[2], pair_ref[3], pair_ref[4]
    return [
        jnp.where(
            (lo <= first_bin + q) & (first_bin + q < hi) & (live > 0), 1.0 / segments, 0.0
        ).astype(jnp.float32)
        for q in range(QUAD)
    ]


def cross_kernel(pair_ref, blocks_ref, out_ref, planes_ref):
    segments = blocks_ref.shape[0] * blocks_ref.shape[4] // QUAD
    groups = blocks_ref.shape[2]
    for g in range(groups):
        first_bin = (pl.program_id(0) * groups + g) * QUAD
        cross_quad(
            blocks_ref[:, 0, g],
            blocks_ref[:, 1, g],
            bin_factors(pair_ref, first_bin, segments),
            planes_ref,
            g * QUAD * 2,
        )
    for a in range(BLK):
        out_ref[a] = planes_ref[pl.ds(a, groups * QUAD * 2, stride=PAD), :].astype(BF)


def cross(pair, blocks):
    sources, _, quads, _, rows, _ = blocks.shape
    groups = 2
    return pl.pallas_call(
        cross_kernel,
        grid=(quads // groups,),
        out_shape=jax.ShapeDtypeStruct((BLK, quads * QUAD * 2, BLK), BF),
        in_specs=[
            pl.BlockSpec(memory_space=pltpu.SMEM),
            pl.BlockSpec((sources, 2, groups, 2, rows, BLK), lambda c: (0, 0, c, 0, 0, 0)),
        ],
        out_specs=pl.BlockSpec((BLK, groups * QUAD * 2, BLK), lambda c: (0, c, 0)),
        scratch_shapes=[pltpu.VMEM((groups * QUAD * 2 * PAD, BLK), jnp.float32)],
    )(pair, blocks)


def lag_kernel(table_ref, cross_ref, out_ref, rows_ref):
    lags, depth = table_ref.shape
    width = cross_ref.shape[0]
    wide = rows_ref.shape[0] // lags
    for a in range(0, width, 2):
        both = jnp.concatenate([cross_ref[a], cross_ref[a + 1]], axis=1)
        lagged = jnp.dot(table_ref[...], both, preferred_element_type=jnp.float32)
        for d in range(2):
            rows_ref[pl.ds(a + d, lags, stride=wide), :] = lagged[:, d * BLK : (d + 1) * BLK]
    out_ref[...] = rows_ref[...].reshape(lags, wide, BLK)[:, :width].astype(BF)


def lag(cross_spec):
    channels, depth, _ = cross_spec.shape
    lags, width = depth, 16
    return pl.pallas_call(
        lag_kernel,
        grid=(channels // width,),
        out_shape=jax.ShapeDtypeStruct((lags, channels, BLK), BF),
        in_specs=[
            pl.BlockSpec((lags, depth), lambda a: (0, 0)),
            pl.BlockSpec((width, depth, BLK), lambda a: (a, 0, 0)),
        ],
        out_specs=pl.BlockSpec((lags, width, BLK), lambda a: (0, a, 0)),
        scratch_shapes=[pltpu.VMEM((lags * (width + 8), BLK), jnp.float32)],
        compiler_params=pltpu.CompilerParams(vmem_limit_bytes=48 << 20),
    )(inverse_table(lags), cross_spec)


def body(strain_rate, pair_table, pair_count):
    whitened = whiten(strain_rate)
    gathered = lax.all_gather(whitened, "band", axis=0, tiled=True)
    band, tm = lax.axis_index("band"), lax.axis_index("tm")
    pairs = lax.dynamic_index_in_dim(pair_table, band, 0, keepdims=False)
    live = (tm < lax.dynamic_index_in_dim(pair_count, band, 0, keepdims=False)).astype(jnp.int32)
    mine = jnp.concatenate([lax.dynamic_index_in_dim(pairs, tm, 0, keepdims=False), live[None]])
    chosen = jnp.take(gathered, pairs[:, :2].reshape(-1), axis=0)
    chosen = chosen.reshape((pairs.shape[0], 2) + whitened.shape[1:])
    blocks = lax.all_to_all(chosen, "tm", split_axis=0, concat_axis=0, tiled=True)
    return lag(cross(mine, blocks))[None, None]


def solution(mesh):
    return jax.shard_map(
        body,
        mesh=mesh,
        in_specs=(P("tm", "band", None), P(), P()),
        out_specs=P("band", "tm", None, None, None),
        check_vma=False,
    )
```

time: 356 us -> 182 us (0.51)
  local copies, waits for them, and re-layouts: 121 us -> 7.7 us
  waiting for transfers between devices: 164 us -> 121 us
  Pallas kernels: 0 us -> 27.6 us
  matrix products: 18.9 us -> 0 us
  blocking collectives: 15.1 us -> 0 us
  loops' own time: 10 us -> 0 us
    all_to_all x1, waiting for transfers between devices: 93.3 us -> 47 us  [body(): lax.all_to_all(chosen, 'tm', split_axis=0, concat_axis=0, tiled=True)]
    gather x32 -> x1, local copies, waits for them, and re-layouts: 36.9 us -> 6.48 us  [body(): chosen = jnp.take(gathered, pairs[:, :2].reshape(-1), axis=0)]
    pallas_call x0 -> x3, Pallas kernels: none -> 27.6 us  [the longest x1 14.5 us: cross(): pl.pallas_call(cross_kernel, grid=(quads // groups,), out_shape=jax.Shape...]
    dynamic_update_slice x16 -> x0, local copies, waits for them, and re-layouts: 21.4 us -> none  [body(): lax.map(per_bin, (gathered, jnp.arange(gathered.shape[0], dtype=jnp.int32)))]
    dot_general x18 -> x0, matrix products: 18.9 us -> none  [the longest x16 10.7 us: cross_block(): jnp.einsum('nsa,nsb->nab', left_rows, right_rows, preferred_element_type=...]
    squeeze x16 -> x0, local copies, waits for them, and re-layouts: 17.3 us -> none  [body(): lax.map(per_bin, (gathered, jnp.arange(gathered.shape[0], dtype=jnp.int32)))]
    all_to_all x1 -> x0, blocking collectives: 15.1 us -> none  [body(): lax.all_to_all(whitened, 'tm', split_axis=0, concat_axis=1, tiled=True)]
    all_to_all x2 -> x0, local copies, waits for them, and re-layouts: 13 us -> none  [the longest x1 12.1 us: body(): lax.all_to_all(cross_spec, 'tm', split_axis=1, concat_axis=0, tiled=True)]
where the time goes in v1:
time: 182 us; the launch traced here: 181 us
  waiting for transfers between devices  121 us (66%)
  Pallas kernels  27.6 us (15%)
  between operations  14 us (8%)
  local copies, waits for them, and re-layouts  7.7 us (4%)
  starting transfers between devices  5.27 us (3%)
  other arithmetic  5.24 us (3%)
    all_gather x1, waiting for transfers between devices, body(): gathered = lax.all_gather(whitened, 'band', axis=0, tiled=True)  74.1 us
    all_to_all x1, waiting for transfers between devices, body(): lax.all_to_all(chosen, 'tm', split_axis=0, concat_axis=0, tiled=True)  47 us
    pallas_call x1, Pallas kernels, cross(): pl.pallas_call(cross_kernel, grid=(quads // groups,), out_shape=jax.Shape...  14.5 us
    pallas_call x1, Pallas kernels, lag(): pl.pallas_call(lag_kernel, grid=(channels // width,), out_shape=jax.Shape...  10.6 us
    gather x1, local copies, waits for them, and re-layouts, body(): chosen = jnp.take(gathered, pairs[:, :2].reshape(-1), axis=0)  6.48 us
    all_to_all x1, starting transfers between devices, body(): lax.all_to_all(chosen, 'tm', split_axis=0, concat_axis=0, tiled=True)  5.27 us
    select_n x2, other arithmetic, body(): chosen = jnp.take(gathered, pairs[:, :2].reshape(-1), axis=0)  4.67 us
  transfers between devices with their start and end apart: 2, of which 2 were waited for; matrix products, arithmetic and copies ran while one was open for 1% of the time, Pallas kernels for 0%

profile of v1, /device:TPU:1, one launch (start us, length us, event | category | flops | bytes accessed | tf_op | source)
XLA Modules:
  0.0 180.9 jit_solution(12546194271238009074)
XLA Ops:
  6.5 0.0 copy-start
  6.5 0.0 all-gather.2.cloned.1.call-start
  6.5 2.4 %shard_map.55 = bf16[2,32,2,16,128]{4,3,2,1,0:T(8,128)(2,1)} custom-call(bf16[4,256,256]{2,1,0:T(8,128)(2,1)} %strain_ref.1, bf16[256,256]{1,0:T(8,128)(2,1)} %constant.61.clone.table_ref), custom_call_target="tpu_custom_call" | custom-call | tf_op jit(solution)/shard_map/pallas_call | solution.py:64
  8.9 0.0 all-gather.2.cloned.1.call-update
  9.0 0.0 copy-done
  9.0 0.1 constant_dynamic-slice_fusion
  9.1 0.1 copy.12
  9.2 0.1 copy.13
  9.3 0.1 copy.14
  9.4 0.1 reshape.42
  9.5 74.1 %all-gather.2.cloned.1.call-done = bf16[32,32,2,16,128]{4,3,2,1,0:T(8,128)(2,1)} async-done(((bf16[2,32,2,16,128]{4,3,2,1,0:T(8,128)(2,1)}), bf16[32,32,2,16,128]{4,3,2,1,0:T(8,128)(2,1)}) %all-gather.2.cloned.1.call-update) | async-done | bytes 8388624 | tf_op jit(solution)/shard_map/all_gather | solution.py:165
  83.6 6.5 %gather_fusion = bf16[16,32,2,16,128]{4,3,2,1,0:T(8,128)(2,1)} fusion(bf16[32,32,2,16,128]{4,3,2,1,0:T(8,128)(2,1)} %all-gather.2.cloned.1.call-done, s32[1024]{0:T(1024)S(1)} %pad_clamp_fusion), kind=kCustom, calls=%fused_computation | custom fusion | bytes 8388672 | tf_op jit(solution)/shard_map/jit(_take)/gather | solution.py:170
  90.1 4.7 %broadcast_select_fusion = bf16[8,2,32,2,16,128]{5,4,3,2,1,0:T(8,128)(2,1)} fusion(bf16[8,2,32,2,16,128]{5,4,3,2,1,0:T(8,128)(2,1)} %bitcast.7, pred[8,2]{1,0:T(8,128)(4,1)S(1)} %copy.13), kind=kLoop, calls=%fused_computation.1 | loop fusion | flops 2097152 | bytes 8388624 | tf_op jit(solution)/shard_map/jit(_take)/select_n | solution.py:170
  94.7 0.0 copy-start.2
  94.7 5.3 %all-to-all-start = ((bf16[8,2,32,2,16,128]{5,4,3,2,1,0:T(8,128)(2,1)}), bf16[8,2,32,2,16,128]{5,4,3,2,1,0:T(8,128)(2,1)}, u32[]{:S(2)}, u32[]{:S(2)}) async-start(bf16[8,2,32,2,16,128]{5,4,3,2,1,0:T(8,128)(2,1)} %broadcast_select_fusion), calls=%async_computation | async-start | bytes 8388608 | tf_op jit(solution)/shard_map/all_to_all | solution.py:172
  100.0 0.0 copy-done.2
  100.0 0.6 dynamic_slice.13
  101.2 0.2 dynamic-slice_reduce_fusion
  101.4 0.6 pad_add_fusion.pair_ref
  101.9 0.0 copy-start.1
  101.9 47.0 %all-to-all-done.blocks_ref = bf16[8,2,32,2,16,128]{5,4,3,2,1,0:T(8,128)(2,1)} async-done(((bf16[8,2,32,2,16,128]{5,4,3,2,1,0:T(8,128)(2,1)}), bf16[8,2,32,2,16,128]{5,4,3,2,1,0:T(8,128)(2,1)}, u32[]{:S(2)}, u32[]{:S(2)}) %all-to-all-start) | async-done | bytes 4194336 | tf_op jit(solution)/shard_map/all_to_all | solution.py:172
  149.0 14.5 %shard_map.56.cross_ref = bf16[128,256,128]{2,1,0:T(8,128)(2,1)} custom-call(s32[5]{0:T(128)} %pad_add_fusion.pair_ref, bf16[8,2,32,2,16,128]{5,4,3,2,1,0:T(8,128)(2,1)} %all-to-all-done.blocks_ref), custom_call_target="tpu_custom_call" | custom-call | tf_op jit(solution)/shard_map/pallas_call | solution.py:121
  163.5 0.0 copy-done.1
  163.5 10.6 %shard_map.57 = bf16[256,128,128]{2,1,0:T(8,128)(2,1)} custom-call(bf16[256,256]{1,0:T(8,128)(2,1)S(1)} %copy-done.1, bf16[128,256,128]{2,1,0:T(8,128)(2,1)} %shard_map.56.cross_ref), custom_call_target="tpu_custom_call" | custom-call | tf_op jit(solution)/shard_map/pallas_call | solution.py:149
  (4 shorter events, 0.0 us)
Async XLA Ops:
  6.5 2.4 %copy-start = (s32[16,8,4]{0,2,1:T(4,128)S(1)}, s32[16,8,4]{0,2,1:T(4,128)}, u32[]{:S(2)}) copy-start(s32[16,8,4]{0,2,1:T(4,128)} %param.6) | copy-start | bytes 6148
  6.5 77.1 %all-gather.2.cloned.1.call-start = ((), (), s32[]{:S(2)}) async-start(), calls=%async_computation.1 | async-start | bytes 8912896 | tf_op jit(solution)/shard_map/all_gather | solution.py:165
  94.7 5.3 %copy-start.2 = (s32[16]{0:T(128)S(1)}, s32[16]{0:T(128)}, u32[]{:S(2)}) copy-start(s32[16]{0:T(128)} %param.7) | copy-start | bytes 196
  94.7 54.2 %all-to-all-start = ((bf16[8,2,32,2,16,128]{5,4,3,2,1,0:T(8,128)(2,1)}), bf16[8,2,32,2,16,128]{5,4,3,2,1,0:T(8,128)(2,1)}, u32[]{:S(2)}, u32[]{:S(2)}) async-start(bf16[8,2,32,2,16,128]{5,4,3,2,1,0:T(8,128)(2,1)} %broadcast_select_fusion), calls=%async_computation | async-start | bytes 8388608 | tf_op jit(solution)/shard_map/all_to_all | solution.py:172
  101.9 61.5 %copy-start.1 = (bf16[256,256]{1,0:T(8,128)(2,1)S(1)}, bf16[256,256]{1,0:T(8,128)(2,1)}, u32[]{:S(2)}) copy-start(bf16[256,256]{1,0:T(8,128)(2,1)} %constant.62.clone.table_ref) | copy-start | bytes 393220
Sparse Core Ops, SparseCore 0:
  9.5 74.0 all-gather.1

commit v2 on v1

--- a/solution.py
+++ b/solution.py
@@ -1,4 +1,3 @@
-import functools
 import math
 
 import jax
@@ -12,7 +11,11 @@
 BLK = 128
 SUB = 64
 EPSILON = 1e-06
+MESH = pl.DeviceIdType.MESH
+SIDE = 4
 QUAD = 4
+GROUPS = 1
+STAGE = (0, 2, 4, 6, 8)
 PAD = 136
 BF = jnp.bfloat16
 
@@ -36,6 +39,7 @@
 
 
 def whiten_kernel(strain_ref, table_ref, out_ref, rows_ref):
+    chunks, _, groups = out_ref.shape[:3]
     segments, channels, samples = strain_ref.shape
     bins = samples // 2
     for g in range(channels // BLK):
@@ -55,7 +59,8 @@
                         part[cut] * scale
                     )
         for r in range(2):
-            out_ref[g, :, r] = rows_ref[r].reshape(bins // QUAD, QUAD * segments, BLK).astype(BF)
+            tiles = rows_ref[r].reshape(chunks, groups, QUAD * segments, BLK)
+            out_ref[:, g, :, r] = tiles.astype(BF)
 
 
 def whiten(strain_rate):
@@ -64,7 +69,7 @@
     return pl.pallas_call(
         whiten_kernel,
         out_shape=jax.ShapeDtypeStruct(
-            (channels // BLK, bins // QUAD, 2, QUAD * segments, BLK), BF
+            (bins // QUAD // GROUPS, channels // BLK, GROUPS, 2, QUAD * segments, BLK), BF
         ),
         in_specs=[pl.BlockSpec(memory_space=pltpu.VMEM)] * 2,
         out_specs=pl.BlockSpec(memory_space=pltpu.VMEM),
@@ -89,8 +94,8 @@
             )
 
 
-def bin_factors(pair_ref, first_bin, segments):
-    lo, hi, live = pair_ref[2], pair_ref[3], pair_ref[4]
+def bin_factors(pair_ref, slot, first_bin, segments):
+    lo, hi, live = pair_ref[slot, 2], pair_ref[slot, 3], pair_ref[slot, 4]
     return [
         jnp.where(
             (lo <= first_bin + q) & (first_bin + q < hi) & (live > 0), 1.0 / segments, 0.0
@@ -99,36 +104,219 @@
     ]
 
 
-def cross_kernel(pair_ref, blocks_ref, out_ref, planes_ref):
-    segments = blocks_ref.shape[0] * blocks_ref.shape[4] // QUAD
-    groups = blocks_ref.shape[2]
-    for g in range(groups):
-        first_bin = (pl.program_id(0) * groups + g) * QUAD
-        cross_quad(
-            blocks_ref[:, 0, g],
-            blocks_ref[:, 1, g],
-            bin_factors(pair_ref, first_bin, segments),
-            planes_ref,
-            g * QUAD * 2,
+def move_kernel(
+    pair_ref, own_ref, out_ref, gat, pick, stage, got, planes, tiles, send, recv, out_sem
+):
+    chunks = own_ref.shape[0]
+    ticks = chunks // 2
+    tm, band = lax.axis_index("tm"), lax.axis_index("band")
+    y, core, x, z = tm // 2, tm % 2, band // SIDE, band % SIDE
+    across = [(1, 0), (3, 0), (2, 0), (1, 1), (3, 1), (2, 1), (0, 1)]
+
+    def along(axis, step):
+        if axis == 0:
+            return (tm, lax.rem(x + step, SIDE) * SIDE + z)
+        return (tm, x * SIDE + lax.rem(z + step, SIDE))
+
+    def over(dy, dc, sign=1):
+        return lax.rem(y + SIDE + sign * dy, SIDE) * 2 + lax.rem(core + dc, 2)
+
+    def block_at(c, axis, step):
+        if axis == 0:
+            return gat.at[c, lax.rem(x + step, SIDE), z]
+        return gat.at[c, x, lax.rem(z + step, SIDE)]
+
+    def line_at(c, axis, step, first, count):
+        if axis == 0:
+            return gat.at[c, lax.rem(x + step, SIDE), pl.ds(first, count)]
+        return gat.at[c, pl.ds(first, count), lax.rem(z + step, SIDE)]
+
+    def copy(src, dst, c, slot, device):
+        return pltpu.make_async_remote_copy(
+            src_ref=src,
+            dst_ref=dst,
+            send_sem=send.at[c, slot],
+            recv_sem=recv.at[c, slot],
+            device_id=device,
+            device_id_type=MESH,
         )
-    for a in range(BLK):
-        out_ref[a] = planes_ref[pl.ds(a, groups * QUAD * 2, stride=PAD), :].astype(BF)
-
-
-def cross(pair, blocks):
-    sources, _, quads, _, rows, _ = blocks.shape
-    groups = 2
+
+    def first(c, axis):
+        out = [
+            (own_ref.at[c], block_at(c, axis, 0), c, k, along(axis, d))
+            for k, d in enumerate((1, 3, 2))
+        ]
+        into = [
+            (own_ref.at[c], block_at(c, axis, SIDE - d), c, k, along(axis, d))
+            for k, d in enumerate((1, 3, 2))
+        ]
+        return out, into
+
+    def second(c, axis):
+        out, into = [], []
+        for k, d in ((3, 1), (4, 3)):
+            mine = line_at(c, axis, 0, 0, SIDE)
+            out.append((mine, mine, c, k, along(axis, d)))
+            theirs = line_at(c, axis, SIDE - d, 0, SIDE)
+            into.append((theirs, theirs, c, k, along(axis, d)))
+        return out, into
+
+    def third(c, axis):
+        out, into = [], []
+        half = SIDE // 2
+        for k, d, at in ((5, 1, 0), (6, 3, half)):
+            passed = line_at(c, axis, SIDE - d, at, half)
+            out.append((passed, passed, c, k, along(axis, d)))
+            theirs = line_at(c, axis, 2, at, half)
+            into.append((theirs, theirs, c, k, along(axis, d)))
+        return out, into
+
+    def last(c):
+        out, into = [], []
+        for k, (dy, dc) in enumerate(across):
+            to, source = over(dy, dc), over(dy, dc, -1)
+            out.append((stage.at[c, to], got.at[c, tm], c, 7 + k, (to, band)))
+            into.append((stage.at[c, to], got.at[c, source], c, 7 + k, (to, band)))
+        return out, into
+
+    def starts(copies):
+        for one in copies:
+            copy(*one).start()
+
+    def arrivals(copies):
+        for one in copies:
+            copy(*one).wait_recv()
+
+    def departures(copies):
+        for one in copies:
+            copy(*one).wait_send()
+
+    def select(c):
+        shape = pick.shape
+        pick[...] = gat[c].reshape(shape)
+        for p in range(stage.shape[1]):
+            for w in range(2):
+                stage[c, p, w] = pick[pair_ref[p, w]]
+        for w in range(2):
+            got[c, tm, w] = pick[pair_ref[tm, w]]
+
+    def write(u, slot):
+        rows = tiles.shape[2]
+        return pltpu.make_async_copy(
+            tiles.at[slot], out_ref.at[:, pl.ds(u * rows, rows), :], out_sem.at[slot]
+        )
+
+    def compute(u):
+        groups = got.shape[3]
+        segments = got.shape[1] * got.shape[5] // QUAD
+        for h in range(2):
+            c = 2 * u + h
+            for g in range(groups):
+                factors = bin_factors(pair_ref, tm, (c * groups + g) * QUAD, segments)
+                cross_quad(
+                    got[c, :, 0, g], got[c, :, 1, g], factors, planes, (h * groups + g) * QUAD * 2
+                )
+        slot = lax.rem(u, 2)
+
+        @pl.when(u >= 2)
+        def _():
+            write(u - 2, slot).wait()
+
+        rows = tiles.shape[2]
+        for a in range(BLK):
+            tiles[slot, a] = planes[pl.ds(a, rows, stride=PAD), :].astype(BF)
+        write(u, slot).start()
+
+    barrier = pltpu.get_barrier_semaphore()
+    partners = [along(axis, d) for axis in (0, 1) for d in (1, 2, 3)]
+    partners += [(over(dy, dc), band) for dy, dc in across]
+    for partner in partners:
+        pl.semaphore_signal(barrier, inc=1, device_id=partner, device_id_type=MESH)
+    pl.semaphore_wait(barrier, len(partners))
+
+    def tick(u, _):
+        def at(lag, act):
+            v = u - lag
+
+            @pl.when((v >= 0) & (v < ticks))
+            def _():
+                act(v)
+
+        def both(act):
+            def run(v):
+                for h in range(2):
+                    act(2 * v + h, h)
+
+            return run
+
+        def begin(c, h):
+            gat[c, x, z] = own_ref[c]
+            starts(first(c, h)[0])
+
+        def spread(c, h):
+            arrivals(first(c, h)[1])
+            starts(second(c, 1 - h)[0])
+
+        def relay(c, h):
+            arrivals(second(c, 1 - h)[1])
+            starts(third(c, 1 - h)[0])
+
+        def cross_over(c, h):
+            arrivals(third(c, 1 - h)[1])
+            select(c)
+            starts(last(c)[0])
+
+        def finish(v):
+            for h in range(2):
+                c = 2 * v + h
+                arrivals(last(c)[1])
+                departures(first(c, h)[0])
+                departures(second(c, 1 - h)[0])
+                departures(third(c, 1 - h)[0])
+                departures(last(c)[0])
+            compute(v)
+
+        at(STAGE[0], both(begin))
+        at(STAGE[1], both(spread))
+        at(STAGE[2], both(relay))
+        at(STAGE[3], both(cross_over))
+        at(STAGE[4], finish)
+        return 0
+
+    lax.fori_loop(0, ticks + STAGE[4], tick, 0)
+    for u in range(ticks - 2, ticks):
+        write(u, u % 2).wait()
+
+
+def move(pairs, own):
+    chunks, blocks, groups, parts, rows, _ = own.shape
+    bands, slots = SIDE * SIDE, pairs.shape[0]
+    tail = (groups, parts, rows, BLK)
+    planes = 2 * groups * QUAD * parts
+    depth = chunks * groups * QUAD * parts
     return pl.pallas_call(
-        cross_kernel,
-        grid=(quads // groups,),
-        out_shape=jax.ShapeDtypeStruct((BLK, quads * QUAD * 2, BLK), BF),
+        move_kernel,
+        out_shape=jax.ShapeDtypeStruct((BLK, depth, BLK), BF),
         in_specs=[
             pl.BlockSpec(memory_space=pltpu.SMEM),
-            pl.BlockSpec((sources, 2, groups, 2, rows, BLK), lambda c: (0, 0, c, 0, 0, 0)),
+            pl.BlockSpec(memory_space=pltpu.VMEM),
         ],
-        out_specs=pl.BlockSpec((BLK, groups * QUAD * 2, BLK), lambda c: (0, c, 0)),
-        scratch_shapes=[pltpu.VMEM((groups * QUAD * 2 * PAD, BLK), jnp.float32)],
-    )(pair, blocks)
+        out_specs=pl.BlockSpec(memory_space=pl.ANY),
+        scratch_shapes=[
+            pltpu.VMEM((chunks, SIDE, SIDE, blocks) + tail, BF),
+            pltpu.VMEM((bands * blocks,) + tail, BF),
+            pltpu.VMEM((chunks, slots, 2) + tail, BF),
+            pltpu.VMEM((chunks, slots, 2) + tail, BF),
+            pltpu.VMEM((planes * PAD, BLK), jnp.float32),
+            pltpu.VMEM((2, BLK, planes, BLK), BF),
+            pltpu.SemaphoreType.DMA((chunks, 14)),
+            pltpu.SemaphoreType.DMA((chunks, 14)),
+            pltpu.SemaphoreType.DMA((2,)),
+        ],
+        compiler_params=pltpu.CompilerParams(
+            collective_id=0, has_side_effects=True, vmem_limit_bytes=48 << 20
+        ),
+    )(pairs, own)
 
 
 def lag_kernel(table_ref, cross_ref, out_ref, rows_ref):
@@ -162,15 +350,12 @@
 
 def body(strain_rate, pair_table, pair_count):
     whitened = whiten(strain_rate)
-    gathered = lax.all_gather(whitened, "band", axis=0, tiled=True)
-    band, tm = lax.axis_index("band"), lax.axis_index("tm")
+    band = lax.axis_index("band")
     pairs = lax.dynamic_index_in_dim(pair_table, band, 0, keepdims=False)
-    live = (tm < lax.dynamic_index_in_dim(pair_count, band, 0, keepdims=False)).astype(jnp.int32)
-    mine = jnp.concatenate([lax.dynamic_index_in_dim(pairs, tm, 0, keepdims=False), live[None]])
-    chosen = jnp.take(gathered, pairs[:, :2].reshape(-1), axis=0)
-    chosen = chosen.reshape((pairs.shape[0], 2) + whitened.shape[1:])
-    blocks = lax.all_to_all(chosen, "tm", split_axis=0, concat_axis=0, tiled=True)
-    return lag(cross(mine, blocks))[None, None]
+    count = lax.dynamic_index_in_dim(pair_count, band, 0, keepdims=False)
+    live = jnp.arange(pairs.shape[0], dtype=jnp.int32) < count
+    pairs = jnp.concatenate([pairs, live[:, None].astype(jnp.int32)], axis=1)
+    return lag(move(pairs, whitened))[None, None]
 
 
 def solution(mesh):

time: 182 us -> 94.7 us (0.52)
  waiting for transfers between devices: 121 us -> 0 us
  Pallas kernels: 27.6 us -> 91 us
  between operations: 14 us -> 0.04 us
  starting transfers between devices: 5.27 us -> 0 us
  local copies, waits for them, and re-layouts: 7.7 us -> 2.59 us
  other arithmetic: 5.24 us -> 0.73 us
    all_gather x1 -> x0, waiting for transfers between devices: 74.1 us -> none  [body(): gathered = lax.all_gather(whitened, 'band', axis=0, tiled=True)]
    pallas_call x2, Pallas kernels: 16.9 us -> 80.3 us  [the longest x1 77.9 us: move(): pl.pallas_call(move_kernel, out_shape=jax.ShapeDtypeStruct((BLK, depth, B...]
    all_to_all x1 -> x0, waiting for transfers between devices: 47 us -> none  [body(): lax.all_to_all(chosen, 'tm', split_axis=0, concat_axis=0, tiled=True)]
    gather x1 -> x0, local copies, waits for them, and re-layouts: 6.48 us -> none  [body(): chosen = jnp.take(gathered, pairs[:, :2].reshape(-1), axis=0)]
    all_to_all x1 -> x0, starting transfers between devices: 5.27 us -> none  [body(): lax.all_to_all(chosen, 'tm', split_axis=0, concat_axis=0, tiled=True)]
    select_n x2 -> x0, other arithmetic: 4.67 us -> none  [body(): chosen = jnp.take(gathered, pairs[:, :2].reshape(-1), axis=0)]
  transfers between devices with their start and end apart: 2 -> 0, of which waited for: 2 -> 0; matrix products, arithmetic and copies ran while one was open for 1% -> 0% of each run, Pallas kernels for 0% -> 0%
where the time goes in v2:
time: 94.7 us; the launch traced here: 94.3 us
  Pallas kernels  91 us (96%)
  local copies, waits for them, and re-layouts  2.59 us (3%)
    pallas_call x1, Pallas kernels, move(): pl.pallas_call(move_kernel, out_shape=jax.ShapeDtypeStruct((BLK, depth, B...  77.9 us
    pallas_call x1, Pallas kernels, lag(): pl.pallas_call(lag_kernel, grid=(channels // width,), out_shape=jax.Shape...  10.6 us
    pallas_call x1, Pallas kernels, whiten(): pl.pallas_call(whiten_kernel, out_shape=jax.ShapeDtypeStruct((bins // QUA...  2.43 us

profile of v2, /device:TPU:1, one launch (start us, length us, event | category | flops | bytes accessed | tf_op | source)
XLA Modules:
  0.0 94.3 jit_solution(5990664566288803765)
XLA Ops:
  0.0 0.0 copy-start
  0.0 0.0 copy-start.2
  0.0 1.3 %dynamic_slice.9 = s32[1]{0:T(128)} dynamic-slice(s32[16]{0:T(128)} %param.7, s32[]{:T(128)S(6)} %select_n.6), dynamic_slice_sizes={1} | dynamic-slice | bytes 12 | tf_op jit(solution)/shard_map/jit(dynamic_index_in_dim)/dynamic_slice | solution.py:355
  1.3 0.6 fusion
  1.9 0.0 copy-done
  1.9 0.1 constant_dynamic-slice_fusion
  2.0 0.1 copy.6
  2.1 0.1 copy.7
  2.2 0.1 pad_add_fusion.pair_ref
  2.3 2.4 %shard_map.55.own_ref = bf16[32,2,1,2,16,128]{5,4,3,2,1,0:T(8,128)(2,1)} custom-call(bf16[4,256,256]{2,1,0:T(8,128)(2,1)} %strain_ref.1, bf16[256,256]{1,0:T(8,128)(2,1)} %constant.18.clone.table_ref), custom_call_target="tpu_custom_call" | custom-call | tf_op jit(solution)/shard_map/pallas_call | solution.py:69
  4.7 0.0 copy-start.1
  4.7 1.0 %copy-done.1 = bf16[32,2,1,2,16,128]{5,4,3,2,1,0:T(8,128)(2,1)S(1)} copy-done((bf16[32,2,1,2,16,128]{5,4,3,2,1,0:T(8,128)(2,1)S(1)}, bf16[32,2,1,2,16,128]{5,4,3,2,1,0:T(8,128)(2,1)}, u32[]{:S(2)}) %copy-start.1) | copy-done | bytes 524312
  5.8 77.9 %shard_map.56.cross_ref = bf16[128,256,128]{2,1,0:T(8,128)(2,1)} custom-call(s32[8,5]{1,0:T(8,128)S(1)} %pad_add_fusion.pair_ref, bf16[32,2,1,2,16,128]{5,4,3,2,1,0:T(8,128)(2,1)S(1)} %copy-done.1), custom_call_target="tpu_custom_call" | custom-call | tf_op jit(solution)/shard_map/pallas_call | solution.py:297
  83.7 0.0 copy-done.2
  83.7 10.6 %shard_map.57 = bf16[256,128,128]{2,1,0:T(8,128)(2,1)} custom-call(bf16[256,256]{1,0:T(8,128)(2,1)S(1)} %copy-done.2, bf16[128,256,128]{2,1,0:T(8,128)(2,1)} %shard_map.56.cross_ref), custom_call_target="tpu_custom_call" | custom-call | tf_op jit(solution)/shard_map/pallas_call | solution.py:337
Async XLA Ops:
  0.0 1.9 %copy-start = (s32[16,8,4]{0,2,1:T(4,128)S(1)}, s32[16,8,4]{0,2,1:T(4,128)}, u32[]{:S(2)}) copy-start(s32[16,8,4]{0,2,1:T(4,128)} %param.6) | copy-start | bytes 6148
  0.0 83.7 %copy-start.2 = (bf16[256,256]{1,0:T(8,128)(2,1)S(1)}, bf16[256,256]{1,0:T(8,128)(2,1)}, u32[]{:S(2)}) copy-start(bf16[256,256]{1,0:T(8,128)(2,1)} %constant.19.clone.table_ref) | copy-start | bytes 393220
  4.7 1.0 %copy-start.1 = (bf16[32,2,1,2,16,128]{5,4,3,2,1,0:T(8,128)(2,1)S(1)}, bf16[32,2,1,2,16,128]{5,4,3,2,1,0:T(8,128)(2,1)}, u32[]{:S(2)}) copy-start(bf16[32,2,1,2,16,128]{5,4,3,2,1,0:T(8,128)(2,1)} %shard_map.55.own_ref) | copy-start | bytes 1572868

commit v3 on v1

--- a/solution.py
+++ b/solution.py
@@ -1,4 +1,3 @@
-import functools
 import math
 
 import jax
@@ -12,6 +11,8 @@
 BLK = 128
 SUB = 64
 EPSILON = 1e-06
+MESH = pl.DeviceIdType.MESH
+SIDE = 4
 QUAD = 4
 PAD = 136
 BF = jnp.bfloat16
@@ -36,6 +37,7 @@
 
 
 def whiten_kernel(strain_ref, table_ref, out_ref, rows_ref):
+    chunks, groups = out_ref.shape[:2]
     segments, channels, samples = strain_ref.shape
     bins = samples // 2
     for g in range(channels // BLK):
@@ -55,7 +57,8 @@
                         part[cut] * scale
                     )
         for r in range(2):
-            out_ref[g, :, r] = rows_ref[r].reshape(bins // QUAD, QUAD * segments, BLK).astype(BF)
+            tiles = rows_ref[r].reshape(chunks, groups, QUAD * segments, BLK)
+            out_ref[:, :, g, r] = tiles.astype(BF)
 
 
 def whiten(strain_rate):
@@ -64,7 +67,7 @@
     return pl.pallas_call(
         whiten_kernel,
         out_shape=jax.ShapeDtypeStruct(
-            (channels // BLK, bins // QUAD, 2, QUAD * segments, BLK), BF
+            (bins // QUAD // SIDE, SIDE, channels // BLK, 2, QUAD * segments, BLK), BF
         ),
         in_specs=[pl.BlockSpec(memory_space=pltpu.VMEM)] * 2,
         out_specs=pl.BlockSpec(memory_space=pltpu.VMEM),
@@ -89,46 +92,217 @@
             )
 
 
-def bin_factors(pair_ref, first_bin, segments):
-    lo, hi, live = pair_ref[2], pair_ref[3], pair_ref[4]
+def bin_factors(pair_ref, band, slot, first_bin, segments):
+    lo, hi = pair_ref[band, slot * 4 + 2], pair_ref[band, slot * 4 + 3]
+    live = slot < pair_ref[band, 32]
     return [
         jnp.where(
-            (lo <= first_bin + q) & (first_bin + q < hi) & (live > 0), 1.0 / segments, 0.0
+            (lo <= first_bin + q) & (first_bin + q < hi) & live, 1.0 / segments, 0.0
         ).astype(jnp.float32)
         for q in range(QUAD)
     ]
 
 
-def cross_kernel(pair_ref, blocks_ref, out_ref, planes_ref):
-    segments = blocks_ref.shape[0] * blocks_ref.shape[4] // QUAD
-    groups = blocks_ref.shape[2]
-    for g in range(groups):
-        first_bin = (pl.program_id(0) * groups + g) * QUAD
-        cross_quad(
-            blocks_ref[:, 0, g],
-            blocks_ref[:, 1, g],
-            bin_factors(pair_ref, first_bin, segments),
-            planes_ref,
-            g * QUAD * 2,
+def move_kernel(
+    pair_ref, own_ref, out_ref, gat, pick, stage, got, planes, tiles, send, recv, out_sem
+):
+    chunks = own_ref.shape[0]
+    ticks = chunks // 2
+    tm, band = lax.axis_index("tm"), lax.axis_index("band")
+    y, core, x, z = tm // 2, tm % 2, band // SIDE, band % SIDE
+    steps = (1, 3, 2)
+    moves = [(dv, dy, dc) for dc in (0, 1) for dv in range(SIDE) for dy in range(SIDE)]
+    moves = [moves[(11 * k) % len(moves)] for k in range(len(moves))]
+    moves = [m for m in moves if m != (0, 0, 0)]
+
+    def around(at, step):
+        return lax.rem(at + step, SIDE)
+
+    def on_line(h, place):
+        return x * SIDE + place if h == 0 else place * SIDE + z
+
+    def on_cross(h, place):
+        return place * SIDE + z if h == 0 else x * SIDE + place
+
+    def mine(h):
+        return (z, x) if h == 0 else (x, z)
+
+    def copy(src, dst, c, slot, device):
+        return pltpu.make_async_remote_copy(
+            src_ref=src,
+            dst_ref=dst,
+            send_sem=send.at[c, slot],
+            recv_sem=recv.at[c, slot],
+            device_id=device,
+            device_id_type=MESH,
         )
-    for a in range(BLK):
-        out_ref[a] = planes_ref[pl.ds(a, groups * QUAD * 2, stride=PAD), :].astype(BF)
-
-
-def cross(pair, blocks):
-    sources, _, quads, _, rows, _ = blocks.shape
-    groups = 2
+
+    def scatter(c, h):
+        out, into = [], []
+        v = mine(h)[0]
+        for k, d in enumerate(steps):
+            to, source = around(v, d), around(v, SIDE - d)
+            there = gat.at[c, x, source] if h == 0 else gat.at[c, source, z]
+            device = (tm, on_line(h, to))
+            out.append((own_ref.at[c, to], gat.at[c, x, z], c, k, device))
+            into.append((own_ref.at[c, to], there, c, k, device))
+        return out, into
+
+    def gather(c, h):
+        out, into = [], []
+        w = mine(h)[1]
+        for k, d in enumerate(steps):
+            here = gat.at[c, x] if h == 0 else gat.at[c, :, z]
+            source = around(w, SIDE - d)
+            there = gat.at[c, source] if h == 0 else gat.at[c, :, source]
+            device = (tm, on_cross(h, around(w, d)))
+            out.append((here, here, c, 3 + k, device))
+            into.append((there, there, c, 3 + k, device))
+        return out, into
+
+    def deal(c, h):
+        out, into = [], []
+        v = mine(h)[0]
+        for k, (dv, dy, dc) in enumerate(moves):
+            to_v, to_t = around(v, dv), around(y, dy) * 2 + lax.rem(core + dc, 2)
+            from_v = around(v, SIDE - dv)
+            from_t = around(y, SIDE - dy) * 2 + lax.rem(core + dc, 2)
+            src, device = stage.at[c, to_v, to_t], (to_t, on_line(h, to_v))
+            out.append((src, got.at[c, v, tm], c, 6 + k, device))
+            into.append((src, got.at[c, from_v, from_t], c, 6 + k, device))
+        return out, into
+
+    def starts(*lists):
+        for group in zip(*lists):
+            for one in group:
+                copy(*one).start()
+
+    def arrivals(copies):
+        for one in copies:
+            copy(*one).wait_recv()
+
+    def departures(copies):
+        for one in copies:
+            copy(*one).wait_send()
+
+    def select(c, h):
+        pick[...] = gat[c].reshape(pick.shape)
+        for v in range(SIDE):
+            owner = on_line(h, v)
+            for p in range(stage.shape[2]):
+                for w in range(2):
+                    stage[c, v, p, w] = pick[pair_ref[owner, p * 4 + w]]
+        for w in range(2):
+            got[c, mine(h)[0], tm, w] = pick[pair_ref[band, tm * 4 + w]]
+
+    def write(c, slot):
+        rows = tiles.shape[2]
+        return pltpu.make_async_copy(
+            tiles.at[slot], out_ref.at[:, pl.ds(c * rows, rows), :], out_sem.at[slot]
+        )
+
+    def compute(c, slot):
+        segments = got.shape[2] * got.shape[5] // QUAD
+        for g in range(SIDE):
+            factors = bin_factors(pair_ref, band, tm, (c * SIDE + g) * QUAD, segments)
+            cross_quad(got[c, g, :, 0], got[c, g, :, 1], factors, planes, g * QUAD * 2)
+
+        @pl.when(c >= 2)
+        def _():
+            write(c - 2, slot).wait()
+
+        rows = tiles.shape[2]
+        for a in range(BLK):
+            tiles[slot, a] = planes[pl.ds(a, rows, stride=PAD), :].astype(BF)
+        write(c, slot).start()
+
+    barrier = pltpu.get_barrier_semaphore()
+    partners = [(tm, on_cross(0, around(x, d))) for d in steps]
+    partners += [(tm, on_cross(1, around(z, d))) for d in steps]
+    for h in range(2):
+        for dv, dy, dc in moves:
+            if dv or h == 0:
+                if (dv, dy, dc) not in ((1, 0, 0), (2, 0, 0), (3, 0, 0)):
+                    to_t = around(y, dy) * 2 + lax.rem(core + dc, 2)
+                    partners.append((to_t, on_line(h, around(mine(h)[0], dv))))
+    for partner in partners:
+        pl.semaphore_signal(barrier, inc=1, device_id=partner, device_id_type=MESH)
+    pl.semaphore_wait(barrier, len(partners))
+
+    def spread(u):
+        for h in range(2):
+            arrivals(scatter(2 * u + h, h)[1])
+        starts(*[gather(2 * u + h, h)[0] for h in range(2)])
+
+    def begin(u, _):
+        for h in range(2):
+            c = 2 * u + h
+            gat[c, x, z] = own_ref[c, mine(h)[0]]
+        starts(*[scatter(2 * u + h, h)[0] for h in range(2)])
+        return 0
+
+    def tick(u, _):
+        @pl.when(u + 1 < ticks)
+        def _():
+            spread(u + 1)
+
+        @pl.when(u < ticks)
+        def _():
+            for h in range(2):
+                arrivals(gather(2 * u + h, h)[1])
+                select(2 * u + h, h)
+            starts(*[deal(2 * u + h, h)[0] for h in range(2)])
+
+        @pl.when(u >= 1)
+        def _():
+            for h in range(2):
+                c = 2 * (u - 1) + h
+                arrivals(deal(c, h)[1])
+                compute(c, h)
+            for h in range(2):
+                c = 2 * (u - 1) + h
+                departures(scatter(c, h)[0])
+                departures(gather(c, h)[0])
+                departures(deal(c, h)[0])
+
+        return 0
+
+    lax.fori_loop(0, ticks, begin, 0)
+    spread(0)
+    lax.fori_loop(0, ticks + 1, tick, 0)
+    for h in range(2):
+        write(chunks - 2 + h, h).wait()
+
+
+def move(pairs, own):
+    chunks, groups, blocks, parts, rows, _ = own.shape
+    bands, slots = SIDE * SIDE, 2 * SIDE
+    tail = (parts, rows, BLK)
+    planes = groups * QUAD * parts
+    depth = chunks * planes
     return pl.pallas_call(
-        cross_kernel,
-        grid=(quads // groups,),
-        out_shape=jax.ShapeDtypeStruct((BLK, quads * QUAD * 2, BLK), BF),
+        move_kernel,
+        out_shape=jax.ShapeDtypeStruct((BLK, depth, BLK), BF),
         in_specs=[
             pl.BlockSpec(memory_space=pltpu.SMEM),
-            pl.BlockSpec((sources, 2, groups, 2, rows, BLK), lambda c: (0, 0, c, 0, 0, 0)),
+            pl.BlockSpec(memory_space=pltpu.VMEM),
         ],
-        out_specs=pl.BlockSpec((BLK, groups * QUAD * 2, BLK), lambda c: (0, c, 0)),
-        scratch_shapes=[pltpu.VMEM((groups * QUAD * 2 * PAD, BLK), jnp.float32)],
-    )(pair, blocks)
+        out_specs=pl.BlockSpec(memory_space=pl.ANY),
+        scratch_shapes=[
+            pltpu.VMEM((chunks, SIDE, SIDE, blocks) + tail, BF),
+            pltpu.VMEM((bands * blocks,) + tail, BF),
+            pltpu.VMEM((chunks, SIDE, slots, 2) + tail, BF),
+            pltpu.VMEM((chunks, groups, slots, 2) + tail, BF),
+            pltpu.VMEM((planes * PAD, BLK), jnp.float32),
+            pltpu.VMEM((2, BLK, planes, BLK), BF),
+            pltpu.SemaphoreType.DMA((chunks, 37)),
+            pltpu.SemaphoreType.DMA((chunks, 37)),
+            pltpu.SemaphoreType.DMA((2,)),
+        ],
+        compiler_params=pltpu.CompilerParams(
+            collective_id=0, has_side_effects=True, vmem_limit_bytes=24 << 20
+        ),
+    )(pairs, own)
 
 
 def lag_kernel(table_ref, cross_ref, out_ref, rows_ref):
@@ -156,21 +330,14 @@
         ],
         out_specs=pl.BlockSpec((lags, width, BLK), lambda a: (0, a, 0)),
         scratch_shapes=[pltpu.VMEM((lags * (width + 8), BLK), jnp.float32)],
-        compiler_params=pltpu.CompilerParams(vmem_limit_bytes=48 << 20),
+        compiler_params=pltpu.CompilerParams(vmem_limit_bytes=24 << 20),
     )(inverse_table(lags), cross_spec)
 
 
 def body(strain_rate, pair_table, pair_count):
     whitened = whiten(strain_rate)
-    gathered = lax.all_gather(whitened, "band", axis=0, tiled=True)
-    band, tm = lax.axis_index("band"), lax.axis_index("tm")
-    pairs = lax.dynamic_index_in_dim(pair_table, band, 0, keepdims=False)
-    live = (tm < lax.dynamic_index_in_dim(pair_count, band, 0, keepdims=False)).astype(jnp.int32)
-    mine = jnp.concatenate([lax.dynamic_index_in_dim(pairs, tm, 0, keepdims=False), live[None]])
-    chosen = jnp.take(gathered, pairs[:, :2].reshape(-1), axis=0)
-    chosen = chosen.reshape((pairs.shape[0], 2) + whitened.shape[1:])
-    blocks = lax.all_to_all(chosen, "tm", split_axis=0, concat_axis=0, tiled=True)
-    return lag(cross(mine, blocks))[None, None]
+    pairs = jnp.concatenate([pair_table.reshape(pair_table.shape[0], -1), pair_count[:, None]], axis=1)
+    return lag(move(pairs, whitened))[None, None]
 
 
 def solution(mesh):

time: 182 us -> 86.7 us (0.48)
  waiting for transfers between devices: 121 us -> 0 us
  Pallas kernels: 27.6 us -> 83.8 us
  between operations: 14 us -> 0.02 us
  starting transfers between devices: 5.27 us -> 0 us
  other arithmetic: 5.24 us -> 0.08 us
  local copies, waits for them, and re-layouts: 7.7 us -> 2.6 us
    all_gather x1 -> x0, waiting for transfers between devices: 74.1 us -> none  [body(): gathered = lax.all_gather(whitened, 'band', axis=0, tiled=True)]
    pallas_call x2, Pallas kernels: 16.9 us -> 76.8 us  [the longest x1 74.3 us: move(): pl.pallas_call(move_kernel, out_shape=jax.ShapeDtypeStruct((BLK, depth, B...]
    all_to_all x1 -> x0, waiting for transfers between devices: 47 us -> none  [body(): lax.all_to_all(chosen, 'tm', split_axis=0, concat_axis=0, tiled=True)]
    gather x1 -> x0, local copies, waits for them, and re-layouts: 6.48 us -> none  [body(): chosen = jnp.take(gathered, pairs[:, :2].reshape(-1), axis=0)]
    all_to_all x1 -> x0, starting transfers between devices: 5.27 us -> none  [body(): lax.all_to_all(chosen, 'tm', split_axis=0, concat_axis=0, tiled=True)]
    select_n x2 -> x0, other arithmetic: 4.67 us -> none  [body(): chosen = jnp.take(gathered, pairs[:, :2].reshape(-1), axis=0)]
    pallas_call x1, Pallas kernels: 10.6 us -> 7.07 us  [lag(): pl.pallas_call(lag_kernel, grid=(channels // width,), out_shape=jax.Shape...]
  transfers between devices with their start and end apart: 2 -> 0, of which waited for: 2 -> 0; matrix products, arithmetic and copies ran while one was open for 1% -> 0% of each run, Pallas kernels for 0% -> 0%
where the time goes in v3:
time: 86.7 us; the launch traced here: 86.5 us
  Pallas kernels  83.8 us (97%)
  local copies, waits for them, and re-layouts  2.6 us (3%)
    pallas_call x1, Pallas kernels, move(): pl.pallas_call(move_kernel, out_shape=jax.ShapeDtypeStruct((BLK, depth, B...  74.3 us
    pallas_call x1, Pallas kernels, lag(): pl.pallas_call(lag_kernel, grid=(channels // width,), out_shape=jax.Shape...  7.07 us
    pallas_call x1, Pallas kernels, whiten(): pl.pallas_call(whiten_kernel, out_shape=jax.ShapeDtypeStruct((bins // QUA...  2.42 us

profile of v3, /device:TPU:1, one launch (start us, length us, event | category | flops | bytes accessed | tf_op | source)
XLA Modules:
  0.0 86.5 jit_solution(5153797517174290644)
XLA Ops:
  0.0 0.0 copy-start.1
  0.0 0.8 copy.8
  0.8 0.7 copy.9
  1.6 0.1 pad_add_fusion.pair_ref
  1.6 2.4 %shard_map.55.own_ref = bf16[8,4,2,2,16,128]{5,4,3,2,1,0:T(8,128)(2,1)} custom-call(bf16[4,256,256]{2,1,0:T(8,128)(2,1)} %strain_ref.1, bf16[256,256]{1,0:T(8,128)(2,1)} %constant.4.clone.table_ref), custom_call_target="tpu_custom_call" | custom-call | tf_op jit(solution)/shard_map/pallas_call | solution.py:67
  4.1 0.0 copy-start
  4.1 1.0 %copy-done = bf16[8,4,2,2,16,128]{5,4,3,2,1,0:T(8,128)(2,1)S(1)} copy-done((bf16[8,4,2,2,16,128]{5,4,3,2,1,0:T(8,128)(2,1)S(1)}, bf16[8,4,2,2,16,128]{5,4,3,2,1,0:T(8,128)(2,1)}, u32[]{:S(2)}) %copy-start) | copy-done | bytes 524312
  5.1 74.3 %shard_map.56.cross_ref = bf16[128,256,128]{2,1,0:T(8,128)(2,1)S(1)} custom-call(s32[16,33]{1,0:T(8,128)S(1)} %pad_add_fusion.pair_ref, bf16[8,4,2,2,16,128]{5,4,3,2,1,0:T(8,128)(2,1)S(1)} %copy-done), custom_call_target="tpu_custom_call" | custom-call | tf_op jit(solution)/shard_map/pallas_call | solution.py:283
  79.4 0.0 copy-done.1
  79.5 7.1 %shard_map.57 = bf16[256,128,128]{2,1,0:T(8,128)(2,1)} custom-call(bf16[256,256]{1,0:T(8,128)(2,1)S(1)} %copy-done.1, bf16[128,256,128]{2,1,0:T(8,128)(2,1)S(1)} %shard_map.56.cross_ref), custom_call_target="tpu_custom_call" | custom-call | tf_op jit(solution)/shard_map/pallas_call | solution.py:323
Async XLA Ops:
  0.0 79.4 %copy-start.1 = (bf16[256,256]{1,0:T(8,128)(2,1)S(1)}, bf16[256,256]{1,0:T(8,128)(2,1)}, u32[]{:S(2)}) copy-start(bf16[256,256]{1,0:T(8,128)(2,1)} %constant.5.clone.table_ref) | copy-start | bytes 393220
  4.1 1.0 %copy-start = (bf16[8,4,2,2,16,128]{5,4,3,2,1,0:T(8,128)(2,1)S(1)}, bf16[8,4,2,2,16,128]{5,4,3,2,1,0:T(8,128)(2,1)}, u32[]{:S(2)}) copy-start(bf16[8,4,2,2,16,128]{5,4,3,2,1,0:T(8,128)(2,1)} %shard_map.55.own_ref) | copy-start | bytes 1572868

commit v4 on v3

v4 whole, which is shorter than its diff:
```python
import math

import jax
import jax.numpy as jnp
import numpy as np
from jax import lax
from jax.experimental import pallas as pl
from jax.experimental.pallas import tpu as pltpu
from jax.sharding import PartitionSpec as P

BLK = 128
SUB = 64
EPSILON = 1e-06
MESH = pl.DeviceIdType.MESH
SIDE = 4
QUAD = 4
PAD = 136
BF = jnp.bfloat16


def forward_table(samples):
    n = np.arange(samples)[None, :]
    k = np.arange(samples // 2)[:, None]
    angles = (n * k % samples) * (2.0 * math.pi / samples)
    factor = 1.0 / math.sqrt(samples)
    table = np.concatenate([np.cos(angles) * factor, -np.sin(angles) * factor], axis=0)
    return jnp.asarray(table.astype(np.float32), dtype=BF)


def inverse_table(samples):
    k = np.arange(samples // 2)[None, :]
    t = np.arange(samples)[:, None]
    angles = (t * k % samples) * (2.0 * math.pi / samples)
    factor = 2.0 / math.sqrt(samples // 2)
    table = np.stack([np.cos(angles) * factor, -np.sin(angles) * factor], axis=2)
    return jnp.asarray(table.reshape(samples, samples).astype(np.float32), dtype=BF)


def whiten(strain_ref, table_ref, own, own_late, rows_ref):
    segments, channels, samples = strain_ref.shape
    bins = samples // 2
    chunks, groups = own.shape[:2]
    early = chunks * groups
    for g in range(channels // BLK):
        for s in range(segments):
            x = strain_ref[s, g * BLK : (g + 1) * BLK, :]
            spec = lax.dot_general(
                table_ref[...], x, (((1,), (1,)), ((), ())), preferred_element_type=jnp.float32
            )
            re, im = spec[:bins], spec[bins:]
            power = re * re + im * im
            for m in range(bins // SUB):
                cut = slice(m * SUB, (m + 1) * SUB)
                level = jnp.mean(power[cut], axis=0, keepdims=True)
                scale = 1.0 / jnp.sqrt(level + EPSILON)
                for r, part in enumerate((re, im)):
                    rows_ref[r, pl.ds(m * SUB * segments + s, SUB, stride=segments), :] = (
                        part[cut] * scale
                    )
        for r in range(2):
            tiles = rows_ref[r].reshape(bins // QUAD, QUAD * segments, BLK).astype(BF)
            own[:, :, g, r] = tiles[:early].reshape(chunks, groups, QUAD * segments, BLK)
            for k in range(early, bins // QUAD):
                own_late[(k - early) * 2 + r, g] = tiles[k]


def cross_quad(left, right, turned, factors, planes_ref, first):
    left_t = left.T
    bin_of = lax.broadcasted_iota(jnp.int32, left_t.shape, 1) % 16 // 4
    stacked = jnp.concatenate(
        [jnp.where(bin_of == q, left_t, jnp.zeros_like(left_t)) for q in range(QUAD)], axis=0
    )
    both = jnp.concatenate([right, turned], axis=1)
    product = jnp.dot(stacked, both, preferred_element_type=jnp.float32)
    for q in range(QUAD):
        for r in range(2):
            planes_ref[pl.ds((first + q * 2 + r) * PAD, BLK), :] = (
                product[q * BLK : (q + 1) * BLK, r * BLK : (r + 1) * BLK] * factors[q]
            )


def bin_factors(pair_ref, count_ref, band, slot, first_bin, segments):
    lo, hi, live = pair_ref[slot, 2, band], pair_ref[slot, 3, band], slot < count_ref[band]
    return [
        jnp.where(
            (lo <= first_bin + q) & (first_bin + q < hi) & live, 1.0 / segments, 0.0
        ).astype(jnp.float32)
        for q in range(QUAD)
    ]


def move_kernel(
    pair_ref, count_ref, strain_ref, table_ref, out_ref, strain, table, rows_ref, own, own_late, gat, late, pick,
    stage, stage_late, got, got_late, planes, tiles, send, recv, send_late, recv_late, load_sem, out_sem,
):
    chunks = own.shape[0]
    tm, band = lax.axis_index("tm"), lax.axis_index("band")
    y, core, x, z = tm // 2, tm % 2, band // SIDE, band % SIDE
    steps = (1, 3, 2)
    moves = [(dv, dy, dc) for dc in (0, 1) for dv in range(SIDE) for dy in range(SIDE)]
    moves = [moves[(11 * k) % len(moves)] for k in range(len(moves))]
    moves = [m for m in moves if m != (0, 0, 0)]

    def around(at, step):
        return lax.rem(at + step, SIDE)

    def on_line(h, place):
        return x * SIDE + place if h == 0 else place * SIDE + z

    def on_cross(h, place):
        return place * SIDE + z if h == 0 else x * SIDE + place

    def mine(h):
        return (z, x) if h == 0 else (x, z)

    def copy(src, dst, c, slot, device):
        return pltpu.make_async_remote_copy(
            src_ref=src,
            dst_ref=dst,
            send_sem=send_late.at[slot] if c is None else send.at[c, slot],
            recv_sem=recv_late.at[slot] if c is None else recv.at[c, slot],
            device_id=device,
            device_id_type=MESH,
        )

    def scatter(c, h):
        out, into = [], []
        v = mine(h)[0]
        for k, d in enumerate(steps):
            to, source = around(v, d), around(v, SIDE - d)
            there = gat.at[c, x, source] if h == 0 else gat.at[c, source, z]
            device = (tm, on_line(h, to))
            out.append((own.at[c, to], gat.at[c, x, z], c, k, device))
            into.append((own.at[c, to], there, c, k, device))
        return out, into

    def gather(c, h):
        out, into = [], []
        w = mine(h)[1]
        for k, d in enumerate(steps):
            here = gat.at[c, x] if h == 0 else gat.at[c, :, z]
            source = around(w, SIDE - d)
            there = gat.at[c, source] if h == 0 else gat.at[c, :, source]
            device = (tm, on_cross(h, around(w, d)))
            out.append((here, here, c, 3 + k, device))
            into.append((there, there, c, 3 + k, device))
        return out, into

    def deal(c, h):
        out, into = [], []
        v = mine(h)[0]
        for k, (dv, dy, dc) in enumerate(moves):
            to_v, to_t = around(v, dv), around(y, dy) * 2 + lax.rem(core + dc, 2)
            from_v = around(v, SIDE - dv)
            from_t = around(y, SIDE - dy) * 2 + lax.rem(core + dc, 2)
            src, device = stage.at[c, to_v, to_t], (to_t, on_line(h, to_v))
            out.append((src, got.at[c, v, tm], c, 6 + k, device))
            into.append((src, got.at[c, from_v, from_t], c, 6 + k, device))
        return out, into

    plane = [(dx, dz) for dz in range(SIDE) for dx in range(SIDE)]
    plane = [plane[(7 * k) % len(plane)] for k in range(len(plane))][1:]

    def scatter_late():
        out, into = [], []
        for k, (dx, dz) in enumerate(plane):
            to = around(x, dx) * SIDE + around(z, dz)
            source = around(x, SIDE - dx) * SIDE + around(z, SIDE - dz)
            here, there = late.at[core, y, pl.ds(band * 2, 2)], late.at[core, y, pl.ds(source * 2, 2)]
            out.append((own_late.at[to], here, None, k, (tm, to)))
            into.append((own_late.at[to], there, None, k, (tm, to)))
        return out, into

    def gather_late():
        out, into = [], []
        for k, d in enumerate(steps):
            here, there = late.at[core, y], late.at[core, around(y, SIDE - d)]
            device = (around(y, d) * 2 + core, band)
            out.append((here, here, None, 15 + k, device))
            into.append((there, there, None, 15 + k, device))
        return out, into

    def swap_late():
        device = (y * 2 + 1 - core, band)
        here, there = late.at[core], late.at[1 - core]
        return [(here, here, None, 18, device)], [(there, there, None, 18, device)]

    def deal_late():
        out, into = [], []
        for k, (dx, dz) in enumerate(plane):
            to = around(x, dx) * SIDE + around(z, dz)
            source = around(x, SIDE - dx) * SIDE + around(z, SIDE - dz)
            out.append((stage_late.at[to], got_late.at[band], None, 19 + k, (tm, to)))
            into.append((stage_late.at[to], got_late.at[source], None, 19 + k, (tm, to)))
        return out, into

    def starts(copies):
        for one in copies:
            copy(*one).start()

    def arrivals(copies):
        for one in copies:
            copy(*one).wait_recv()

    def departures(copies):
        for one in copies:
            copy(*one).wait_send()

    def select(c, h):
        pick[...] = gat[c].reshape(pick.shape)
        for v in range(SIDE):
            owner = on_line(h, v)
            for p in range(stage.shape[2]):
                for w in range(2):
                    stage[c, v, p, w] = pick[pair_ref[p, w, owner]]
        for w in range(2):
            got[c, mine(h)[0], tm, w] = pick[pair_ref[tm, w, band]]

    def select_late():
        for owner in range(SIDE * SIDE):
            for w in range(2):
                stage_late[owner, w] = late[:, :, pair_ref[tm, w, owner]]
        got_late[band] = stage_late[band]

    def write(c, slot):
        rows = tiles.shape[2]
        return pltpu.make_async_copy(
            tiles.at[slot], out_ref.at[:, pl.ds(c * rows, rows), :], out_sem.at[slot]
        )

    def compute(c, after, blocks_of):
        slot = lax.rem(c, 2)
        segments = got.shape[2] * got.shape[5] // QUAD
        for g in range(SIDE):
            factors = bin_factors(pair_ref, count_ref, band, tm, (c * SIDE + g) * QUAD, segments)
            cross_quad(*blocks_of(g), factors, planes, g * QUAD * 2)

        if after is not None:
            write(after, slot).wait()
        rows = tiles.shape[2]
        for a in range(BLK):
            tiles[slot, a] = planes[pl.ds(a, rows, stride=PAD), :].astype(BF)
        write(c, slot).start()

    def chunk_blocks(c):
        def blocks_of(g):
            left, right = got[c, g, :, 0], got[c, g, :, 1]
            turned = jnp.stack([-right[:, 1], right[:, 0]], axis=1)
            return [b.reshape(-1, BLK) for b in (left, right, turned)]

        return blocks_of

    def late_blocks(first):
        def blocks_of(g):
            piece = (first + g) * 2
            left = jnp.stack([got_late[piece, 0], got_late[piece + 1, 0]])
            right = jnp.stack([got_late[piece, 1], got_late[piece + 1, 1]])
            turned = jnp.stack([-right[1], right[0]])
            return [b.reshape(-1, BLK) for b in (left, right, turned)]

        return blocks_of

    loads = [
        pltpu.make_async_copy(strain_ref, strain, load_sem.at[0]),
        pltpu.make_async_copy(table_ref, table, load_sem.at[1]),
    ]
    for load in loads:
        load.start()
    barrier = pltpu.get_barrier_semaphore()
    partners = [(tm, around(x, dx) * SIDE + around(z, dz)) for dx, dz in plane]
    for h in range(2):
        for dv, dy, dc in moves:
            if (dv or h == 0) and (dy or dc):
                to_t = around(y, dy) * 2 + lax.rem(core + dc, 2)
                partners.append((to_t, on_line(h, around(mine(h)[0], dv))))
    for partner in partners:
        pl.semaphore_signal(barrier, inc=1, device_id=partner, device_id_type=MESH)
    for load in loads:
        load.wait()
    whiten(strain, table, own, own_late, rows_ref)
    pl.semaphore_wait(barrier, len(partners))

    def begin(u):
        for h in range(2):
            c = 2 * u + h
            gat[c, x, z] = own[c, mine(h)[0]]
            starts(scatter(c, h)[0])

    def spread(u):
        for h in range(2):
            c = 2 * u + h
            arrivals(scatter(c, h)[1])
            starts(gather(c, h)[0])

    def send_out(u, extra):
        for h in range(2):
            c = 2 * u + h
            arrivals(gather(c, h)[1])
            select(c, h)
            copies = deal(c, h)[0]
            mixed = []
            for k, one in enumerate(copies):
                mixed.append(one)
                mixed += extra[h][k * len(extra[h]) // len(copies) : (k + 1) * len(extra[h]) // len(copies)]
            starts(mixed)

    def finish(u):
        for h in range(2):
            c = 2 * u + h
            arrivals(deal(c, h)[1])
            compute(c, c - 2 if u else None, chunk_blocks(c))

    def settle(u):
        for h in range(2):
            c = 2 * u + h
            departures(scatter(c, h)[0])
            departures(gather(c, h)[0])
            departures(deal(c, h)[0])

    begin(0)
    late[core, y, pl.ds(band * 2, 2)] = own_late[band]
    starts(scatter_late()[0])
    begin(1)
    begin(2)
    spread(0)
    arrivals(scatter_late()[1])
    starts(gather_late()[0])
    send_out(0, ([], []))
    spread(1)
    arrivals(gather_late()[1])
    starts(swap_late()[0])
    spread(2)
    arrivals(swap_late()[1])
    select_late()
    rest = deal_late()[0]
    send_out(1, (rest[0:4], rest[4:8]))
    finish(0)
    send_out(2, (rest[8:11], rest[11:15]))
    settle(0)
    departures(scatter_late()[0])
    departures(gather_late()[0])
    departures(swap_late()[0])
    finish(1)
    settle(1)
    arrivals(deal_late()[1])
    for k in range(2):
        compute(chunks + k, chunks - 4 + k, late_blocks(SIDE * k))
    departures(deal_late()[0])
    for h in range(2):
        c = chunks - 2 + h
        arrivals(deal(c, h)[1])
        compute(c, chunks + h, chunk_blocks(c))
    settle(2)
    for h in range(2):
        write(chunks - 2 + h, h).wait()


def move(pairs, counts, strain_rate):
    segments, channels, samples = strain_rate.shape
    bins, blocks, slots, bands = samples // 2, channels // BLK, 2 * SIDE, SIDE * SIDE
    rows, parts, planes = QUAD * segments, 2, SIDE * QUAD * 2
    pieces = bands
    chunks = (bins // QUAD - pieces // parts) // SIDE
    tile = (rows, BLK)
    return pl.pallas_call(
        move_kernel,
        out_shape=jax.ShapeDtypeStruct((BLK, bins * parts, BLK), BF),
        in_specs=[pl.BlockSpec(memory_space=pltpu.SMEM)] * 2
        + [pl.BlockSpec(memory_space=pl.ANY)] * 2,
        out_specs=pl.BlockSpec(memory_space=pl.ANY),
        scratch_shapes=[
            pltpu.VMEM(strain_rate.shape, BF),
            pltpu.VMEM((samples, samples), BF),
            pltpu.VMEM((parts, bins * segments, BLK), jnp.float32),
            pltpu.VMEM((chunks, SIDE, blocks, parts) + tile, BF),
            pltpu.VMEM((pieces, blocks) + tile, BF),
            pltpu.VMEM((chunks, SIDE, SIDE, blocks, parts) + tile, BF),
            pltpu.VMEM((2, SIDE, bands * blocks) + tile, BF),
            pltpu.VMEM((bands * blocks, parts) + tile, BF),
            pltpu.VMEM((chunks, SIDE, slots, 2, parts) + tile, BF),
            pltpu.VMEM((bands, 2, 2, SIDE) + tile, BF),
            pltpu.VMEM((chunks, SIDE, slots, 2, parts) + tile, BF),
            pltpu.VMEM((pieces, 2, 2, SIDE) + tile, BF),
            pltpu.VMEM((planes * PAD, BLK), jnp.float32),
            pltpu.VMEM((2, BLK, planes, BLK), BF),
            pltpu.SemaphoreType.DMA((chunks, 37)),
            pltpu.SemaphoreType.DMA((chunks, 37)),
            pltpu.SemaphoreType.DMA((34,)),
            pltpu.SemaphoreType.DMA((34,)),
            pltpu.SemaphoreType.DMA((2,)),
            pltpu.SemaphoreType.DMA((2,)),
        ],
        compiler_params=pltpu.CompilerParams(
            collective_id=0, has_side_effects=True, vmem_limit_bytes=24 << 20
        ),
    )(pairs, counts, strain_rate, forward_table(samples))


def lag_kernel(table_ref, cross_ref, out_ref, rows_ref):
    lags, depth = table_ref.shape
    width = cross_ref.shape[0]
    wide = rows_ref.shape[0] // lags
    for a in range(0, width, 2):
        both = jnp.concatenate([cross_ref[a], cross_ref[a + 1]], axis=1)
        lagged = jnp.dot(table_ref[...], both, preferred_element_type=jnp.float32)
        for d in range(2):
            rows_ref[pl.ds(a + d, lags, stride=wide), :] = lagged[:, d * BLK : (d + 1) * BLK]
    out_ref[...] = rows_ref[...].reshape(lags, wide, BLK)[:, :width].astype(BF)


def lag(cross_spec):
    channels, depth, _ = cross_spec.shape
    lags, width = depth, 16
    return pl.pallas_call(
        lag_kernel,
        grid=(channels // width,),
        out_shape=jax.ShapeDtypeStruct((lags, channels, BLK), BF),
        in_specs=[
            pl.BlockSpec((lags, depth), lambda a: (0, 0)),
            pl.BlockSpec((width, depth, BLK), lambda a: (a, 0, 0)),
        ],
        out_specs=pl.BlockSpec((lags, width, BLK), lambda a: (0, a, 0)),
        scratch_shapes=[pltpu.VMEM((lags * (width + 8), BLK), jnp.float32)],
        compiler_params=pltpu.CompilerParams(vmem_limit_bytes=24 << 20),
    )(inverse_table(lags), cross_spec)


def body(strain_rate, pair_table, pair_count):
    pairs = jnp.transpose(pair_table, (1, 2, 0))
    return lag(move(pairs, pair_count, strain_rate))[None, None]


def solution(mesh):
    return jax.shard_map(
        body,
        mesh=mesh,
        in_specs=(P("tm", "band", None), P(), P()),
        out_specs=P("band", "tm", None, None, None),
        check_vma=False,
    )
```

time: 86.7 us -> 77.2 us (0.89)
  Pallas kernels: 83.8 us -> 73.6 us
    pallas_call x2 -> x1, Pallas kernels: 76.8 us -> 66.5 us  [move(): pl.pallas_call(move_kernel, out_shape=jax.ShapeDtypeStruct((BLK, bins * p...]
    unnamed x4 -> x10, local copies, waits for them, and re-layouts: 1.04 us -> 3.32 us
where the time goes in v4:
time: 77.2 us; the launch traced here: 77 us
  Pallas kernels  73.6 us (95%)
  local copies, waits for them, and re-layouts  3.32 us (4%)
    pallas_call x1, Pallas kernels, move(): pl.pallas_call(move_kernel, out_shape=jax.ShapeDtypeStruct((BLK, bins * p...  66.5 us
    pallas_call x1, Pallas kernels, lag(): pl.pallas_call(lag_kernel, grid=(channels // width,), out_shape=jax.Shape...  7.11 us
    unnamed x10, local copies, waits for them, and re-layouts  3.32 us

profile of v4, /device:TPU:1, one launch (start us, length us, event | category | flops | bytes accessed | tf_op | source)
XLA Modules:
  0.0 77.0 jit_solution(14134982123766379430)
XLA Ops:
  0.0 0.0 copy-start
  0.0 1.0 %copy-done = bf16[4,256,256]{2,1,0:T(8,128)(2,1)S(1)} copy-done((bf16[4,256,256]{2,1,0:T(8,128)(2,1)S(1)}, bf16[4,256,256]{2,1,0:T(8,128)(2,1)}, u32[]{:S(2)}) %copy-start) | copy-done | bytes 524312
  1.0 0.0 copy-start.1
  1.0 0.9 %copy-done.1 = bf16[256,256]{1,0:T(8,128)(2,1)S(1)} copy-done((bf16[256,256]{1,0:T(8,128)(2,1)S(1)}, bf16[256,256]{1,0:T(8,128)(2,1)}, u32[]{:S(2)}) %copy-start.1) | copy-done | bytes 131096
  1.9 0.0 copy-start.3
  1.9 0.7 copy-done.3
  2.7 0.0 copy-start.4
  2.7 0.7 copy-done.4
  3.3 0.0 copy-start.2
  3.3 66.5 %shard_map.55.cross_ref = bf16[128,256,128]{2,1,0:T(8,128)(2,1)S(1)} custom-call(s32[8,4,16]{2,1,0:T(4,128)S(1)} %bitcast.2, s32[16]{0:T(128)S(1)} %copy-done.4, bf16[4,256,256]{2,1,0:T(8,128)(2,1)S(1)} %copy-done, bf16[256,256]{1,0:T(8,128)(2,1)S(1)} %copy-done.1), custom_call_target="tpu_custom_call" | custom-call | tf_op jit(solution)/shard_map/pallas_call | solution.py:365
  69.8 0.0 copy-done.2
  69.8 7.1 %shard_map.56 = bf16[256,128,128]{2,1,0:T(8,128)(2,1)} custom-call(bf16[256,256]{1,0:T(8,128)(2,1)S(1)} %copy-done.2, bf16[128,256,128]{2,1,0:T(8,128)(2,1)S(1)} %shard_map.55.cross_ref), custom_call_target="tpu_custom_call" | custom-call | tf_op jit(solution)/shard_map/pallas_call | solution.py:414
Async XLA Ops:
  0.0 1.0 %copy-start = (bf16[4,256,256]{2,1,0:T(8,128)(2,1)S(1)}, bf16[4,256,256]{2,1,0:T(8,128)(2,1)}, u32[]{:S(2)}) copy-start(bf16[4,256,256]{2,1,0:T(8,128)(2,1)} %strain_ref.1) | copy-start | bytes 1572868
  1.0 0.9 %copy-start.1 = (bf16[256,256]{1,0:T(8,128)(2,1)S(1)}, bf16[256,256]{1,0:T(8,128)(2,1)}, u32[]{:S(2)}) copy-start(bf16[256,256]{1,0:T(8,128)(2,1)} %constant.4.clone.table_ref) | copy-start | bytes 393220
  1.9 0.7 copy-start.3
  2.7 0.7 copy-start.4
  3.3 66.5 %copy-start.2 = (bf16[256,256]{1,0:T(8,128)(2,1)S(1)}, bf16[256,256]{1,0:T(8,128)(2,1)}, u32[]{:S(2)}) copy-start(bf16[256,256]{1,0:T(8,128)(2,1)} %constant.5.clone.table_ref) | copy-start | bytes 393220

commit v5 on v4

--- a/solution.py
+++ b/solution.py
@@ -317,14 +317,14 @@
             departures(gather(c, h)[0])
             departures(deal(c, h)[0])
 
-    begin(0)
     late[core, y, pl.ds(band * 2, 2)] = own_late[band]
     starts(scatter_late()[0])
+    begin(0)
+    arrivals(scatter_late()[1])
+    starts(gather_late()[0])
+    spread(0)
     begin(1)
     begin(2)
-    spread(0)
-    arrivals(scatter_late()[1])
-    starts(gather_late()[0])
     send_out(0, ([], []))
     spread(1)
     arrivals(gather_late()[1])
@@ -333,9 +333,9 @@
     arrivals(swap_late()[1])
     select_late()
     rest = deal_late()[0]
-    send_out(1, (rest[0:4], rest[4:8]))
+    send_out(1, (rest[0:8], rest[8:15]))
     finish(0)
-    send_out(2, (rest[8:11], rest[11:15]))
+    send_out(2, ([], []))
     settle(0)
     departures(scatter_late()[0])
     departures(gather_late()[0])
@@ -396,16 +396,37 @@
     )(pairs, counts, strain_rate, forward_table(samples))
 
 
-def lag_kernel(table_ref, cross_ref, out_ref, rows_ref):
-    lags, depth = table_ref.shape
-    width = cross_ref.shape[0]
+def lag_kernel(table_ref, cross_ref, out_ref, rows_ref, tiles, out_sem):
+    lags = table_ref.shape[0]
+    channels, width = cross_ref.shape[0], tiles.shape[2]
     wide = rows_ref.shape[0] // lags
-    for a in range(0, width, 2):
-        both = jnp.concatenate([cross_ref[a], cross_ref[a + 1]], axis=1)
-        lagged = jnp.dot(table_ref[...], both, preferred_element_type=jnp.float32)
-        for d in range(2):
-            rows_ref[pl.ds(a + d, lags, stride=wide), :] = lagged[:, d * BLK : (d + 1) * BLK]
-    out_ref[...] = rows_ref[...].reshape(lags, wide, BLK)[:, :width].astype(BF)
+    steps = channels // width
+
+    def write(i, slot):
+        return pltpu.make_async_copy(
+            tiles.at[slot], out_ref.at[:, pl.ds(i * width, width), :], out_sem.at[slot]
+        )
+
+    def step(i, _):
+        slot = lax.rem(i, 2)
+        for a in range(0, width, 2):
+            at = i * width + a
+            both = jnp.concatenate([cross_ref[at], cross_ref[at + 1]], axis=1)
+            lagged = jnp.dot(table_ref[...], both, preferred_element_type=jnp.float32)
+            for d in range(2):
+                rows_ref[pl.ds(a + d, lags, stride=wide), :] = lagged[:, d * BLK : (d + 1) * BLK]
+
+        @pl.when(i >= 2)
+        def _():
+            write(i - 2, slot).wait()
+
+        tiles[slot] = rows_ref[...].reshape(lags, wide, BLK)[:, :width].astype(BF)
+        write(i, slot).start()
+        return 0
+
+    lax.fori_loop(0, steps, step, 0)
+    for i in range(steps - 2, steps):
+        write(i, i % 2).wait()
 
 
 def lag(cross_spec):
@@ -413,14 +434,14 @@
     lags, width = depth, 16
     return pl.pallas_call(
         lag_kernel,
-        grid=(channels // width,),
         out_shape=jax.ShapeDtypeStruct((lags, channels, BLK), BF),
-        in_specs=[
-            pl.BlockSpec((lags, depth), lambda a: (0, 0)),
-            pl.BlockSpec((width, depth, BLK), lambda a: (a, 0, 0)),
+        in_specs=[pl.BlockSpec(memory_space=pltpu.VMEM)] * 2,
+        out_specs=pl.BlockSpec(memory_space=pl.ANY),
+        scratch_shapes=[
+            pltpu.VMEM((lags * (width + 8), BLK), jnp.float32),
+            pltpu.VMEM((2, lags, width, BLK), BF),
+            pltpu.SemaphoreType.DMA((2,)),
         ],
-        out_specs=pl.BlockSpec((lags, width, BLK), lambda a: (0, a, 0)),
-        scratch_shapes=[pltpu.VMEM((lags * (width + 8), BLK), jnp.float32)],
         compiler_params=pltpu.CompilerParams(vmem_limit_bytes=24 << 20),
     )(inverse_table(lags), cross_spec)
 

time: 77.2 us -> 73.5 us (0.952)
  Pallas kernels: 73.6 us -> 69.9 us
    pallas_call x1, Pallas kernels: 66.5 us -> 63.4 us  [move(): pl.pallas_call(move_kernel, out_shape=jax.ShapeDtypeStruct((BLK, bins * p...]
where the time goes in v5:
time: 73.5 us; the launch traced here: 73.3 us
  Pallas kernels  69.9 us (95%)
  local copies, waits for them, and re-layouts  3.32 us (5%)
    pallas_call x1, Pallas kernels, move(): pl.pallas_call(move_kernel, out_shape=jax.ShapeDtypeStruct((BLK, bins * p...  63.4 us
    pallas_call x1, Pallas kernels, lag(): pl.pallas_call(lag_kernel, out_shape=jax.ShapeDtypeStruct((lags, channels...  6.49 us
    unnamed x10, local copies, waits for them, and re-layouts  3.32 us

profile of v5, /device:TPU:1, one launch (start us, length us, event | category | flops | bytes accessed | tf_op | source)
XLA Modules:
  0.0 73.3 jit_solution(12931002919455140812)
XLA Ops:
  0.0 0.0 copy-start
  0.0 1.0 %copy-done = bf16[4,256,256]{2,1,0:T(8,128)(2,1)S(1)} copy-done((bf16[4,256,256]{2,1,0:T(8,128)(2,1)S(1)}, bf16[4,256,256]{2,1,0:T(8,128)(2,1)}, u32[]{:S(2)}) %copy-start) | copy-done | bytes 524312
  1.0 0.0 copy-start.1
  1.0 0.9 %copy-done.1 = bf16[256,256]{1,0:T(8,128)(2,1)S(1)} copy-done((bf16[256,256]{1,0:T(8,128)(2,1)S(1)}, bf16[256,256]{1,0:T(8,128)(2,1)}, u32[]{:S(2)}) %copy-start.1) | copy-done | bytes 131096
  1.9 0.0 copy-start.3
  1.9 0.7 copy-done.3
  2.7 0.0 copy-start.4
  2.7 0.7 copy-done.4
  3.3 0.0 copy-start.2
  3.3 63.4 %shard_map.55.cross_ref = bf16[128,256,128]{2,1,0:T(8,128)(2,1)S(1)} custom-call(s32[8,4,16]{2,1,0:T(4,128)S(1)} %bitcast.2, s32[16]{0:T(128)S(1)} %copy-done.4, bf16[4,256,256]{2,1,0:T(8,128)(2,1)S(1)} %copy-done, bf16[256,256]{1,0:T(8,128)(2,1)S(1)} %copy-done.1), custom_call_target="tpu_custom_call" | custom-call | tf_op jit(solution)/shard_map/pallas_call | solution.py:365
  66.8 0.0 copy-done.2
  66.8 6.5 %shard_map.56 = bf16[256,128,128]{2,1,0:T(8,128)(2,1)} custom-call(bf16[256,256]{1,0:T(8,128)(2,1)S(1)} %copy-done.2, bf16[128,256,128]{2,1,0:T(8,128)(2,1)S(1)} %shard_map.55.cross_ref), custom_call_target="tpu_custom_call" | custom-call | tf_op jit(solution)/shard_map/pallas_call | solution.py:435
Async XLA Ops:
  0.0 1.0 %copy-start = (bf16[4,256,256]{2,1,0:T(8,128)(2,1)S(1)}, bf16[4,256,256]{2,1,0:T(8,128)(2,1)}, u32[]{:S(2)}) copy-start(bf16[4,256,256]{2,1,0:T(8,128)(2,1)} %strain_ref.1) | copy-start | bytes 1572868
  1.0 0.9 %copy-start.1 = (bf16[256,256]{1,0:T(8,128)(2,1)S(1)}, bf16[256,256]{1,0:T(8,128)(2,1)}, u32[]{:S(2)}) copy-start(bf16[256,256]{1,0:T(8,128)(2,1)} %constant.4.clone.table_ref) | copy-start | bytes 393220
  1.9 0.7 copy-start.3
  2.7 0.7 copy-start.4
  3.3 63.5 %copy-start.2 = (bf16[256,256]{1,0:T(8,128)(2,1)S(1)}, bf16[256,256]{1,0:T(8,128)(2,1)}, u32[]{:S(2)}) copy-start(bf16[256,256]{1,0:T(8,128)(2,1)} %constant.5.clone.table_ref) | copy-start | bytes 393220

commit v6 on v5

--- a/solution.py
+++ b/solution.py
@@ -93,7 +93,7 @@
     pair_ref, count_ref, strain_ref, table_ref, out_ref, strain, table, rows_ref, own, own_late, gat, late, pick,
     stage, stage_late, got, got_late, planes, tiles, send, recv, send_late, recv_late, load_sem, out_sem,
 ):
-    chunks = own.shape[0]
+    chunks, slots = own.shape[0], pair_ref.shape[0]
     tm, band = lax.axis_index("tm"), lax.axis_index("band")
     y, core, x, z = tm // 2, tm % 2, band // SIDE, band % SIDE
     steps = (1, 3, 2)
@@ -124,97 +124,79 @@
         )
 
     def scatter(c, h):
-        out, into = [], []
         v = mine(h)[0]
-        for k, d in enumerate(steps):
-            to, source = around(v, d), around(v, SIDE - d)
-            there = gat.at[c, x, source] if h == 0 else gat.at[c, source, z]
-            device = (tm, on_line(h, to))
-            out.append((own.at[c, to], gat.at[c, x, z], c, k, device))
-            into.append((own.at[c, to], there, c, k, device))
-        return out, into
+        tos = [around(v, d) for d in steps]
+        return [(own.at[c, to], gat.at[c, x, z], c, 0, (tm, on_line(h, to))) for to in tos]
 
     def gather(c, h):
-        out, into = [], []
-        w = mine(h)[1]
-        for k, d in enumerate(steps):
-            here = gat.at[c, x] if h == 0 else gat.at[c, :, z]
-            source = around(w, SIDE - d)
-            there = gat.at[c, source] if h == 0 else gat.at[c, :, source]
-            device = (tm, on_cross(h, around(w, d)))
-            out.append((here, here, c, 3 + k, device))
-            into.append((there, there, c, 3 + k, device))
-        return out, into
+        here = gat.at[c, x] if h == 0 else gat.at[c, :, z]
+        return [
+            (here, here, c, 1, (tm, on_cross(h, around(mine(h)[1], d)))) for d in steps
+        ]
 
     def deal(c, h):
-        out, into = [], []
+        out = []
         v = mine(h)[0]
-        for k, (dv, dy, dc) in enumerate(moves):
+        for dv, dy, dc in moves:
             to_v, to_t = around(v, dv), around(y, dy) * 2 + lax.rem(core + dc, 2)
-            from_v = around(v, SIDE - dv)
-            from_t = around(y, SIDE - dy) * 2 + lax.rem(core + dc, 2)
-            src, device = stage.at[c, to_v, to_t], (to_t, on_line(h, to_v))
-            out.append((src, got.at[c, v, tm], c, 6 + k, device))
-            into.append((src, got.at[c, from_v, from_t], c, 6 + k, device))
-        return out, into
+            src, dst = stage.at[c, to_v * slots + to_t], got.at[c, v * slots + tm]
+            out.append((src, dst, c, 2, (to_t, on_line(h, to_v))))
+        return out
 
     plane = [(dx, dz) for dz in range(SIDE) for dx in range(SIDE)]
     plane = [plane[(7 * k) % len(plane)] for k in range(len(plane))][1:]
+    over = [around(x, dx) * SIDE + around(z, dz) for dx, dz in plane]
 
     def scatter_late():
-        out, into = [], []
-        for k, (dx, dz) in enumerate(plane):
-            to = around(x, dx) * SIDE + around(z, dz)
-            source = around(x, SIDE - dx) * SIDE + around(z, SIDE - dz)
-            here, there = late.at[core, y, pl.ds(band * 2, 2)], late.at[core, y, pl.ds(source * 2, 2)]
-            out.append((own_late.at[to], here, None, k, (tm, to)))
-            into.append((own_late.at[to], there, None, k, (tm, to)))
-        return out, into
+        here = late.at[core, y, pl.ds(band * 2, 2)]
+        return [(own_late.at[to], here, None, 0, (tm, to)) for to in over]
 
     def gather_late():
-        out, into = [], []
-        for k, d in enumerate(steps):
-            here, there = late.at[core, y], late.at[core, around(y, SIDE - d)]
-            device = (around(y, d) * 2 + core, band)
-            out.append((here, here, None, 15 + k, device))
-            into.append((there, there, None, 15 + k, device))
-        return out, into
+        here = late.at[core, y]
+        return [(here, here, None, 1, (around(y, d) * 2 + core, band)) for d in steps]
 
     def swap_late():
-        device = (y * 2 + 1 - core, band)
-        here, there = late.at[core], late.at[1 - core]
-        return [(here, here, None, 18, device)], [(there, there, None, 18, device)]
+        here = late.at[core]
+        return [(here, here, None, 2, (y * 2 + 1 - core, band))]
 
     def deal_late():
-        out, into = [], []
-        for k, (dx, dz) in enumerate(plane):
-            to = around(x, dx) * SIDE + around(z, dz)
-            source = around(x, SIDE - dx) * SIDE + around(z, SIDE - dz)
-            out.append((stage_late.at[to], got_late.at[band], None, 19 + k, (tm, to)))
-            into.append((stage_late.at[to], got_late.at[source], None, 19 + k, (tm, to)))
-        return out, into
+        return [(stage_late.at[to], got_late.at[band], None, 3, (tm, to)) for to in over]
 
     def starts(copies):
         for one in copies:
             copy(*one).start()
 
-    def arrivals(copies):
-        for one in copies:
-            copy(*one).wait_recv()
-
-    def departures(copies):
-        for one in copies:
-            copy(*one).wait_send()
+    def size(c, k):
+        if c is None:
+            return (
+                own_late.at[pl.ds(0, len(over))],
+                late.at[0, pl.ds(0, SIDE - 1)],
+                late.at[0],
+                stage_late.at[pl.ds(0, len(over))],
+            )[k]
+        return (
+            own.at[c, pl.ds(0, SIDE - 1)],
+            gat.at[c, pl.ds(0, SIDE - 1)],
+            stage.at[c, pl.ds(0, len(moves))],
+        )[k]
+
+    def arrivals(c, k):
+        sem = recv_late.at[k] if c is None else recv.at[c, k]
+        pltpu.make_async_copy(size(c, k), size(c, k), sem).wait()
+
+    def departures(c, k):
+        sem = send_late.at[k] if c is None else send.at[c, k]
+        pltpu.make_async_copy(size(c, k), size(c, k), sem).wait()
 
     def select(c, h):
         pick[...] = gat[c].reshape(pick.shape)
         for v in range(SIDE):
             owner = on_line(h, v)
-            for p in range(stage.shape[2]):
+            for p in range(slots):
                 for w in range(2):
-                    stage[c, v, p, w] = pick[pair_ref[p, w, owner]]
+                    stage[c, v * slots + p, w] = pick[pair_ref[p, w, owner]]
         for w in range(2):
-            got[c, mine(h)[0], tm, w] = pick[pair_ref[tm, w, band]]
+            got[c, mine(h)[0] * slots + tm, w] = pick[pair_ref[tm, w, band]]
 
     def select_late():
         for owner in range(SIDE * SIDE):
@@ -230,7 +212,7 @@
 
     def compute(c, after, blocks_of):
         slot = lax.rem(c, 2)
-        segments = got.shape[2] * got.shape[5] // QUAD
+        segments = slots * got.shape[4] // QUAD
         for g in range(SIDE):
             factors = bin_factors(pair_ref, count_ref, band, tm, (c * SIDE + g) * QUAD, segments)
             cross_quad(*blocks_of(g), factors, planes, g * QUAD * 2)
@@ -244,7 +226,8 @@
 
     def chunk_blocks(c):
         def blocks_of(g):
-            left, right = got[c, g, :, 0], got[c, g, :, 1]
+            here = pl.ds(g * slots, slots)
+            left, right = got[c, here, 0], got[c, here, 1]
             turned = jnp.stack([-right[:, 1], right[:, 0]], axis=1)
             return [b.reshape(-1, BLK) for b in (left, right, turned)]
 
@@ -267,7 +250,7 @@
     for load in loads:
         load.start()
     barrier = pltpu.get_barrier_semaphore()
-    partners = [(tm, around(x, dx) * SIDE + around(z, dz)) for dx, dz in plane]
+    partners = [(tm, to) for to in over]
     for h in range(2):
         for dv, dy, dc in moves:
             if (dv or h == 0) and (dy or dc):
@@ -284,20 +267,20 @@
         for h in range(2):
             c = 2 * u + h
             gat[c, x, z] = own[c, mine(h)[0]]
-            starts(scatter(c, h)[0])
+            starts(scatter(c, h))
 
     def spread(u):
         for h in range(2):
             c = 2 * u + h
-            arrivals(scatter(c, h)[1])
-            starts(gather(c, h)[0])
+            arrivals(c, 0)
+            starts(gather(c, h))
 
     def send_out(u, extra):
         for h in range(2):
             c = 2 * u + h
-            arrivals(gather(c, h)[1])
+            arrivals(c, 1)
             select(c, h)
-            copies = deal(c, h)[0]
+            copies = deal(c, h)
             mixed = []
             for k, one in enumerate(copies):
                 mixed.append(one)
@@ -307,48 +290,47 @@
     def finish(u):
         for h in range(2):
             c = 2 * u + h
-            arrivals(deal(c, h)[1])
+            arrivals(c, 2)
             compute(c, c - 2 if u else None, chunk_blocks(c))
 
     def settle(u):
         for h in range(2):
             c = 2 * u + h
-            departures(scatter(c, h)[0])
-            departures(gather(c, h)[0])
-            departures(deal(c, h)[0])
+            for k in range(3):
+                departures(c, k)
 
     late[core, y, pl.ds(band * 2, 2)] = own_late[band]
-    starts(scatter_late()[0])
+    starts(scatter_late())
     begin(0)
-    arrivals(scatter_late()[1])
-    starts(gather_late()[0])
+    arrivals(None, 0)
+    starts(gather_late())
     spread(0)
     begin(1)
     begin(2)
     send_out(0, ([], []))
     spread(1)
-    arrivals(gather_late()[1])
-    starts(swap_late()[0])
+    arrivals(None, 1)
+    starts(swap_late())
     spread(2)
-    arrivals(swap_late()[1])
+    arrivals(None, 2)
     select_late()
-    rest = deal_late()[0]
+    rest = deal_late()
     send_out(1, (rest[0:8], rest[8:15]))
     finish(0)
     send_out(2, ([], []))
     settle(0)
-    departures(scatter_late()[0])
-    departures(gather_late()[0])
-    departures(swap_late()[0])
+    departures(None, 0)
+    departures(None, 1)
+    departures(None, 2)
     finish(1)
     settle(1)
-    arrivals(deal_late()[1])
+    arrivals(None, 3)
     for k in range(2):
         compute(chunks + k, chunks - 4 + k, late_blocks(SIDE * k))
-    departures(deal_late()[0])
+    departures(None, 3)
     for h in range(2):
         c = chunks - 2 + h
-        arrivals(deal(c, h)[1])
+        arrivals(c, 2)
         compute(c, chunks + h, chunk_blocks(c))
     settle(2)
     for h in range(2):
@@ -377,16 +359,16 @@
             pltpu.VMEM((chunks, SIDE, SIDE, blocks, parts) + tile, BF),
             pltpu.VMEM((2, SIDE, bands * blocks) + tile, BF),
             pltpu.VMEM((bands * blocks, parts) + tile, BF),
-            pltpu.VMEM((chunks, SIDE, slots, 2, parts) + tile, BF),
+            pltpu.VMEM((chunks, SIDE * slots, 2, parts) + tile, BF),
             pltpu.VMEM((bands, 2, 2, SIDE) + tile, BF),
-            pltpu.VMEM((chunks, SIDE, slots, 2, parts) + tile, BF),
+            pltpu.VMEM((chunks, SIDE * slots, 2, parts) + tile, BF),
             pltpu.VMEM((pieces, 2, 2, SIDE) + tile, BF),
             pltpu.VMEM((planes * PAD, BLK), jnp.float32),
             pltpu.VMEM((2, BLK, planes, BLK), BF),
-            pltpu.SemaphoreType.DMA((chunks, 37)),
-            pltpu.SemaphoreType.DMA((chunks, 37)),
-            pltpu.SemaphoreType.DMA((34,)),
-            pltpu.SemaphoreType.DMA((34,)),
+            pltpu.SemaphoreType.DMA((chunks, 3)),
+            pltpu.SemaphoreType.DMA((chunks, 3)),
+            pltpu.SemaphoreType.DMA((4,)),
+            pltpu.SemaphoreType.DMA((4,)),
             pltpu.SemaphoreType.DMA((2,)),
             pltpu.SemaphoreType.DMA((2,)),
         ],

time: 73.5 us -> 69 us (0.939)
  Pallas kernels: 69.9 us -> 65 us
    pallas_call x1, Pallas kernels: 63.4 us -> 58.5 us  [move(): pl.pallas_call(move_kernel, out_shape=jax.ShapeDtypeStruct((BLK, bins * p...]
where the time goes in v6:
time: 69 us; the launch traced here: 68.3 us
  Pallas kernels  65 us (94%)
  local copies, waits for them, and re-layouts  3.32 us (5%)
    pallas_call x1, Pallas kernels, move(): pl.pallas_call(move_kernel, out_shape=jax.ShapeDtypeStruct((BLK, bins * p...  58.5 us
    pallas_call x1, Pallas kernels, lag(): pl.pallas_call(lag_kernel, out_shape=jax.ShapeDtypeStruct((lags, channels...  6.49 us
    unnamed x10, local copies, waits for them, and re-layouts  3.32 us

profile of v6, /device:TPU:1, one launch (start us, length us, event | category | flops | bytes accessed | tf_op | source)
XLA Modules:
  0.0 68.3 jit_solution(6667781728099847881)
XLA Ops:
  0.0 0.0 copy-start
  0.0 1.0 %copy-done = bf16[4,256,256]{2,1,0:T(8,128)(2,1)S(1)} copy-done((bf16[4,256,256]{2,1,0:T(8,128)(2,1)S(1)}, bf16[4,256,256]{2,1,0:T(8,128)(2,1)}, u32[]{:S(2)}) %copy-start) | copy-done | bytes 524312
  1.0 0.0 copy-start.1
  1.0 0.9 %copy-done.1 = bf16[256,256]{1,0:T(8,128)(2,1)S(1)} copy-done((bf16[256,256]{1,0:T(8,128)(2,1)S(1)}, bf16[256,256]{1,0:T(8,128)(2,1)}, u32[]{:S(2)}) %copy-start.1) | copy-done | bytes 131096
  1.9 0.0 copy-start.3
  1.9 0.7 %copy-done.3 = s32[16,8,4]{0,2,1:T(4,128)S(1)} copy-done((s32[16,8,4]{0,2,1:T(4,128)S(1)}, s32[16,8,4]{0,2,1:T(4,128)}, u32[]{:S(2)}) %copy-start.3) | copy-done | bytes 2072
  2.7 0.0 copy-start.4
  2.7 0.7 copy-done.4
  3.3 0.0 copy-start.2
  3.3 58.5 %shard_map.55.cross_ref = bf16[128,256,128]{2,1,0:T(8,128)(2,1)S(1)} custom-call(s32[8,4,16]{2,1,0:T(4,128)S(1)} %bitcast.2, s32[16]{0:T(128)S(1)} %copy-done.4, bf16[4,256,256]{2,1,0:T(8,128)(2,1)S(1)} %copy-done, bf16[256,256]{1,0:T(8,128)(2,1)S(1)} %copy-done.1), custom_call_target="tpu_custom_call" | custom-call | tf_op jit(solution)/shard_map/pallas_call | solution.py:347
  61.8 0.0 copy-done.2
  61.8 6.5 %shard_map.56 = bf16[256,128,128]{2,1,0:T(8,128)(2,1)} custom-call(bf16[256,256]{1,0:T(8,128)(2,1)S(1)} %copy-done.2, bf16[128,256,128]{2,1,0:T(8,128)(2,1)S(1)} %shard_map.55.cross_ref), custom_call_target="tpu_custom_call" | custom-call | tf_op jit(solution)/shard_map/pallas_call | solution.py:417
Async XLA Ops:
  0.0 1.0 %copy-start = (bf16[4,256,256]{2,1,0:T(8,128)(2,1)S(1)}, bf16[4,256,256]{2,1,0:T(8,128)(2,1)}, u32[]{:S(2)}) copy-start(bf16[4,256,256]{2,1,0:T(8,128)(2,1)} %strain_ref.1) | copy-start | bytes 1572868
  1.0 0.9 %copy-start.1 = (bf16[256,256]{1,0:T(8,128)(2,1)S(1)}, bf16[256,256]{1,0:T(8,128)(2,1)}, u32[]{:S(2)}) copy-start(bf16[256,256]{1,0:T(8,128)(2,1)} %constant.4.clone.table_ref) | copy-start | bytes 393220
  1.9 0.7 %copy-start.3 = (s32[16,8,4]{0,2,1:T(4,128)S(1)}, s32[16,8,4]{0,2,1:T(4,128)}, u32[]{:S(2)}) copy-start(s32[16,8,4]{0,2,1:T(4,128)} %param.6) | copy-start | bytes 6148
  2.7 0.7 copy-start.4
  3.3 58.5 %copy-start.2 = (bf16[256,256]{1,0:T(8,128)(2,1)S(1)}, bf16[256,256]{1,0:T(8,128)(2,1)}, u32[]{:S(2)}) copy-start(bf16[256,256]{1,0:T(8,128)(2,1)} %constant.5.clone.table_ref) | copy-start | bytes 393220

commit v7 on v6

--- a/solution.py
+++ b/solution.py
@@ -90,8 +90,8 @@
 
 
 def move_kernel(
-    pair_ref, count_ref, strain_ref, table_ref, out_ref, strain, table, rows_ref, own, own_late, gat, late, pick,
-    stage, stage_late, got, got_late, planes, tiles, send, recv, send_late, recv_late, load_sem, out_sem,
+    pair_ref, count_ref, strain_ref, table_ref, out_ref, rows_ref, own, own_late, gat, late, pick,
+    stage, stage_late, got, got_late, planes, tiles, send, recv, send_late, recv_late, out_sem,
 ):
     chunks, slots = own.shape[0], pair_ref.shape[0]
     tm, band = lax.axis_index("tm"), lax.axis_index("band")
@@ -243,12 +243,6 @@
 
         return blocks_of
 
-    loads = [
-        pltpu.make_async_copy(strain_ref, strain, load_sem.at[0]),
-        pltpu.make_async_copy(table_ref, table, load_sem.at[1]),
-    ]
-    for load in loads:
-        load.start()
     barrier = pltpu.get_barrier_semaphore()
     partners = [(tm, to) for to in over]
     for h in range(2):
@@ -258,9 +252,7 @@
                 partners.append((to_t, on_line(h, around(mine(h)[0], dv))))
     for partner in partners:
         pl.semaphore_signal(barrier, inc=1, device_id=partner, device_id_type=MESH)
-    for load in loads:
-        load.wait()
-    whiten(strain, table, own, own_late, rows_ref)
+    whiten(strain_ref, table_ref, own, own_late, rows_ref)
     pl.semaphore_wait(barrier, len(partners))
 
     def begin(u):
@@ -348,11 +340,9 @@
         move_kernel,
         out_shape=jax.ShapeDtypeStruct((BLK, bins * parts, BLK), BF),
         in_specs=[pl.BlockSpec(memory_space=pltpu.SMEM)] * 2
-        + [pl.BlockSpec(memory_space=pl.ANY)] * 2,
+        + [pl.BlockSpec(memory_space=pltpu.VMEM)] * 2,
         out_specs=pl.BlockSpec(memory_space=pl.ANY),
         scratch_shapes=[
-            pltpu.VMEM(strain_rate.shape, BF),
-            pltpu.VMEM((samples, samples), BF),
             pltpu.VMEM((parts, bins * segments, BLK), jnp.float32),
             pltpu.VMEM((chunks, SIDE, blocks, parts) + tile, BF),
             pltpu.VMEM((pieces, blocks) + tile, BF),
@@ -370,7 +360,6 @@
             pltpu.SemaphoreType.DMA((4,)),
             pltpu.SemaphoreType.DMA((4,)),
             pltpu.SemaphoreType.DMA((2,)),
-            pltpu.SemaphoreType.DMA((2,)),
         ],
         compiler_params=pltpu.CompilerParams(
             collective_id=0, has_side_effects=True, vmem_limit_bytes=24 << 20

time: 69 us -> 68.8 us (level)
  no operation moved by 1% of the time
where the time goes in v7:
time: 68.8 us; the launch traced here: 68.1 us
  Pallas kernels  64.8 us (94%)
  local copies, waits for them, and re-layouts  3.32 us (5%)
    pallas_call x1, Pallas kernels, move(): pl.pallas_call(move_kernel, out_shape=jax.ShapeDtypeStruct((BLK, bins * p...  58.3 us
    pallas_call x1, Pallas kernels, lag(): pl.pallas_call(lag_kernel, out_shape=jax.ShapeDtypeStruct((lags, channels...  6.49 us
    unnamed x10, local copies, waits for them, and re-layouts  3.32 us

profile of v7, /device:TPU:1, one launch (start us, length us, event | category | flops | bytes accessed | tf_op | source)
XLA Modules:
  0.0 68.1 jit_solution(2689722940698002968)
XLA Ops:
  0.0 0.0 copy-start
  0.0 1.0 %copy-done = bf16[4,256,256]{2,1,0:T(8,128)(2,1)S(1)} copy-done((bf16[4,256,256]{2,1,0:T(8,128)(2,1)S(1)}, bf16[4,256,256]{2,1,0:T(8,128)(2,1)}, u32[]{:S(2)}) %copy-start) | copy-done | bytes 524312
  1.0 0.0 copy-start.1
  1.0 0.9 %copy-done.1 = bf16[256,256]{1,0:T(8,128)(2,1)S(1)} copy-done((bf16[256,256]{1,0:T(8,128)(2,1)S(1)}, bf16[256,256]{1,0:T(8,128)(2,1)}, u32[]{:S(2)}) %copy-start.1) | copy-done | bytes 131096
  1.9 0.0 copy-start.3
  1.9 0.7 %copy-done.3 = s32[16,8,4]{0,2,1:T(4,128)S(1)} copy-done((s32[16,8,4]{0,2,1:T(4,128)S(1)}, s32[16,8,4]{0,2,1:T(4,128)}, u32[]{:S(2)}) %copy-start.3) | copy-done | bytes 2072
  2.7 0.0 copy-start.4
  2.7 0.7 copy-done.4
  3.3 0.0 copy-start.2
  3.3 58.3 %shard_map.55.cross_ref = bf16[128,256,128]{2,1,0:T(8,128)(2,1)S(1)} custom-call(s32[8,4,16]{2,1,0:T(4,128)S(1)} %bitcast.2, s32[16]{0:T(128)S(1)} %copy-done.4, bf16[4,256,256]{2,1,0:T(8,128)(2,1)S(1)} %copy-done, bf16[256,256]{1,0:T(8,128)(2,1)S(1)} %copy-done.1), custom_call_target="tpu_custom_call" | custom-call | tf_op jit(solution)/shard_map/pallas_call | solution.py:339
  61.6 0.0 copy-done.2
  61.6 6.5 %shard_map.56 = bf16[256,128,128]{2,1,0:T(8,128)(2,1)} custom-call(bf16[256,256]{1,0:T(8,128)(2,1)S(1)} %copy-done.2, bf16[128,256,128]{2,1,0:T(8,128)(2,1)S(1)} %shard_map.55.cross_ref), custom_call_target="tpu_custom_call" | custom-call | tf_op jit(solution)/shard_map/pallas_call | solution.py:406
Async XLA Ops:
  0.0 1.0 %copy-start = (bf16[4,256,256]{2,1,0:T(8,128)(2,1)S(1)}, bf16[4,256,256]{2,1,0:T(8,128)(2,1)}, u32[]{:S(2)}) copy-start(bf16[4,256,256]{2,1,0:T(8,128)(2,1)} %strain_ref.1) | copy-start | bytes 1572868
  1.0 0.9 %copy-start.1 = (bf16[256,256]{1,0:T(8,128)(2,1)S(1)}, bf16[256,256]{1,0:T(8,128)(2,1)}, u32[]{:S(2)}) copy-start(bf16[256,256]{1,0:T(8,128)(2,1)} %constant.4.clone.table_ref) | copy-start | bytes 393220
  1.9 0.7 %copy-start.3 = (s32[16,8,4]{0,2,1:T(4,128)S(1)}, s32[16,8,4]{0,2,1:T(4,128)}, u32[]{:S(2)}) copy-start(s32[16,8,4]{0,2,1:T(4,128)} %param.6) | copy-start | bytes 6148
  2.7 0.7 copy-start.4
  3.3 58.3 %copy-start.2 = (bf16[256,256]{1,0:T(8,128)(2,1)S(1)}, bf16[256,256]{1,0:T(8,128)(2,1)}, u32[]{:S(2)}) copy-start(bf16[256,256]{1,0:T(8,128)(2,1)} %constant.5.clone.table_ref) | copy-start | bytes 393220
